TPU v7x, 256 devices: a whole 4x4x8 slice. The times are simulated.
256 devices in a mesh: seq: 16 (over y, x), head: 16 (over z, core).
Axes of the slice: x: 4, y: 4, z: 8, core: 2. Of those that a mesh axis runs over, the one named last changes fastest.
Arguments:
- inputs: bfloat16 [81920, 8192], P(('seq', 'head')), may hold values from -0.15625 to 0.15625
- log_decay: float32 [81920, 128], P(('seq', 'head')), may hold values from -2 to 0, as said below
- write_vectors: bfloat16 [81920, 1024], P(('seq', 'head')), may hold values from -6 to 6
- read_vectors: bfloat16 [81920, 1024], P(('seq', 'head')), may hold values from -0.5 to 0.5
Outputs:
- mixed: bfloat16 [81920, 8192], P(('seq', 'head'))
Inputs may be any that keep to these rules, and one draw needn't show every extreme that they name: `log_decay`: every entry is negative.
All inputs are finite; a program needn't handle non-finite values.
Results may differ from a plain program's by a relative error of at most 0.0056.
Values may be sent and summed in bfloat16 or wider, within the bound.
No kernel may reach another device: no remote copies, remote signals or barrier semaphores. Data moves between devices by JAX's collectives and lax.ppermute only.
A program may use at most 128 MiB of HBM per device.

v0:
```python
import jax
import jax.numpy as jnp
from jax import lax
from jax.sharding import PartitionSpec as P

G = 8
SPAN = 256


def carried_in(part, axis, combine, identity):
    place = lax.axis_index(axis)
    gathered = jax.tree.map(lambda a: lax.all_gather(a, axis), part)
    state = jax.tree.map(lambda a, e: jnp.zeros_like(a) + jnp.asarray(e, a.dtype), part, identity)

    def one(step, state):
        return combine(
            state, jax.tree.map(lambda a: lax.dynamic_index_in_dim(a, step, 0, False), gathered)
        )

    return lax.fori_loop(0, place, one, state)


def block_terms(block):
    block_x, block_b, block_c, block_a = block
    cumulative = jnp.cumsum(block_a, axis=0)
    scores = jnp.einsum("in,jn->ij", block_c, block_b, preferred_element_type=jnp.float32)
    length = block_a.shape[0]
    order = jnp.arange(length, dtype=jnp.int32)
    lower = order[:, None] >= order[None, :]
    cum_heads = cumulative.T
    spread = jnp.where(lower[None], cum_heads[:, :, None] - cum_heads[:, None, :], -jnp.inf)
    weights = (scores[None] * jnp.exp(spread)).astype(jnp.bfloat16)
    diagonal = jnp.einsum("hij,jhp->ihp", weights, block_x, preferred_element_type=jnp.float32)
    fading = jnp.exp(cumulative[-1][None, :] - cumulative)
    scaled = (fading[:, :, None] * block_b[:, None, :].astype(jnp.float32)).astype(jnp.bfloat16)
    contribution = jnp.einsum("jhn,jhp->hnp", scaled, block_x, preferred_element_type=jnp.float32)
    return (diagonal, contribution, cumulative)


def combine_states(earlier, later):
    return (earlier[0] + later[0], jnp.exp(later[0])[:, None, None] * earlier[1] + later[1])


def shards(inputs, log_decay, write_vectors, read_vectors):
    heads_all = log_decay.shape[1]
    head_devices = lax.axis_size("head")
    local_rows = inputs.shape[0]
    heads_dev = heads_all // head_devices
    channels = inputs.shape[1] // heads_all
    state_size = write_vectors.shape[1] // G
    copies = head_devices // G
    features = inputs.reshape(local_rows, head_devices, heads_dev * channels)
    writers = jnp.repeat(write_vectors.reshape(local_rows, G, state_size), copies, axis=1)
    readers = jnp.repeat(read_vectors.reshape(local_rows, G, state_size), copies, axis=1)
    features, writers, readers = (
        lax.all_to_all(features, "head", split_axis=1, concat_axis=0, tiled=True),
        lax.all_to_all(writers, "head", split_axis=1, concat_axis=0, tiled=True),
        lax.all_to_all(readers, "head", split_axis=1, concat_axis=0, tiled=True),
    )
    decays = lax.all_to_all(
        log_decay.reshape(local_rows, head_devices, heads_dev),
        "head",
        split_axis=1,
        concat_axis=0,
        tiled=True,
    )
    partition_tokens = local_rows * head_devices
    spans = partition_tokens // SPAN
    blocked_x = features.reshape(spans, SPAN, heads_dev, channels)
    blocked_b = writers.reshape(spans, SPAN, state_size)
    blocked_c = readers.reshape(spans, SPAN, state_size)
    blocked_a = decays.reshape(spans, SPAN, heads_dev)
    diagonal, contribution, cumulative = lax.map(
        block_terms, (blocked_x, blocked_b, blocked_c, blocked_a)
    )
    span_ends = cumulative[:, -1, :]

    def advance(carry, item):
        start, before = carry
        end_decay, term = item
        return (
            (jnp.exp(end_decay)[:, None, None] * start + term, before + end_decay),
            (start, before),
        )

    empty_state = jnp.zeros((heads_dev, state_size, channels), jnp.float32)
    empty_decay = jnp.zeros((heads_dev,), jnp.float32)
    (final_state, whole_decay), (starts, befores) = lax.scan(
        advance, (empty_state, empty_decay), (span_ends, contribution)
    )
    _, entry = carried_in(
        (whole_decay, final_state), "seq", combine_states, (empty_decay, empty_state)
    )
    held = (starts + jnp.exp(befores)[:, :, None, None] * entry[None]).astype(jnp.bfloat16)
    read_projection = jnp.einsum(
        "cin,chnp->cihp", blocked_c, held, preferred_element_type=jnp.float32
    )
    read_projection = read_projection * jnp.exp(cumulative)[:, :, :, None]
    result = (diagonal + read_projection).astype(jnp.bfloat16)
    result = result.reshape(head_devices, local_rows, heads_dev * channels)
    returned = lax.all_to_all(result, "head", split_axis=0, concat_axis=2, tiled=True)
    return returned.reshape(local_rows, heads_all * channels)


def solution(mesh):
    in_specs = (
        P(("seq", "head"), None),
        P(("seq", "head"), None),
        P(("seq", "head"), None),
        P(("seq", "head"), None),
    )
    out_specs = P(("seq", "head"), None)
    return jax.shard_map(shards, mesh=mesh, in_specs=in_specs, out_specs=out_specs, check_vma=False)
```

profile of v0, /device:TPU:31, one launch (start us, length us, event | category | flops | bytes accessed | tf_op | source)
XLA Modules:
  0.0 673.8 jit_solution(5606855396436315105)
XLA Ops:
  8.3 9.2 %all-to-all-start.3 = ((f32[320,16,8]{0,2,1:T(8,128)}), f32[320,16,8]{0,2,1:T(8,128)S(1)}, u32[]{:S(2)}, u32[]{:S(2)}) async-start(f32[320,16,8]{0,2,1:T(8,128)} %bitcast.25), calls=%async_computation.3 | async-start | bytes 393216 | tf_op jit(solution)/shard_map/all_to_all | solution.py:60
  17.6 10.2 %all-to-all-done.3 = f32[320,16,8]{0,2,1:T(8,128)S(1)} async-done(((f32[320,16,8]{0,2,1:T(8,128)}), f32[320,16,8]{0,2,1:T(8,128)S(1)}, u32[]{:S(2)}, u32[]{:S(2)}) %all-to-all-start.3) | async-done | bytes 163872 | tf_op jit(solution)/shard_map/all_to_all | solution.py:60
  29.1 3.6 all-to-all-start.1
  32.7 5.4 copy.92
  38.2 27.3 %all-to-all-done.1 = bf16[320,16,128]{2,0,1:T(8,128)(2,1)S(1)} async-done(((bf16[320,16,128]{2,0,1:T(8,128)(2,1)}), bf16[320,16,128]{2,0,1:T(8,128)(2,1)S(1)}, u32[]{:S(2)}, u32[]{:S(2)}) %all-to-all-start.1) | async-done | bytes 1310752 | tf_op jit(solution)/shard_map/all_to_all | solution.py:58
  65.5 4.6 all-to-all-start
  70.3 115.4 %all-to-all-done = bf16[320,16,512]{2,0,1:T(8,128)(2,1)} async-done(((bf16[320,16,512]{2,0,1:T(8,128)(2,1)}), bf16[320,16,512]{2,0,1:T(8,128)(2,1)}, u32[]{:S(2)}, u32[]{:S(2)}) %all-to-all-start) | async-done | bytes 5242912 | tf_op jit(solution)/shard_map/all_to_all | solution.py:56
  186.9 5.5 all-to-all-start.2
  192.7 13.9 %reshape.128 = bf16[20,256,8,64]{3,2,1,0:T(8,128)(2,1)} reshape(bf16[16,320,1,512]{3,1,0,2:T(8,128)(2,1)} %bitcast.16) | data formatting | bytes 10485760 | tf_op jit(solution)/shard_map/reshape | solution.py:69
  206.6 11.1 %copy.63 = bf16[20,256,8,64]{1,3,2,0:T(8,128)(2,1)} copy(bf16[20,256,8,64]{3,2,1,0:T(8,128)(2,1)} %reshape.128) | data formatting | bytes 10485760 | tf_op jit(solution)/shard_map/while | solution.py:73
  217.7 8.0 %all-to-all-done.2 = bf16[320,16,128]{2,0,1:T(8,128)(2,1)} async-done(((bf16[320,16,128]{2,0,1:T(8,128)(2,1)}), bf16[320,16,128]{2,0,1:T(8,128)(2,1)}, u32[]{:S(2)}, u32[]{:S(2)}) %all-to-all-start.2) | async-done | bytes 1310752 | tf_op jit(solution)/shard_map/all_to_all | solution.py:57
  225.7 154.1 %while.43 = (s32[]{:T(128)}, f32[20,256,8,64]{1,3,2,0:T(8,128)}, f32[20,8,128,64]{2,3,1,0:T(8,128)}, f32[20,256,8]{1,2,0:T(8,128)S(1)}, bf16[20,256,8,64]{1,3,2,...) while((s32[]{:T(128)}, f32[20,256,8,64]{1,3,2,0:T(8,128)}, ...), condition=%wide.region_3.4_spmd, body=%wide.region_0.3_spmd.sunk | while | flops 120426520 | bytes 2560697 | solution.py:73
  227.7 2.4 fusion.47
  258.5 2.4 fusion.47
  266.3 2.4 fusion.47
  382.8 44.4 %while.45 = (s32[]{:T(128)}, f32[8,128,64]{2,1,0:T(8,128)S(1)}, f32[8]{0:T(128)S(1)}, f32[20,8,128,64]{3,2,1,0:T(8,128)}, f32[20,8]{1,0:T(8,128)S(1)}, /*index=5...) while((s32[]{:T(128)}, f32[8,128,64]{2,1,0:T(8,128)S(1)}, ...), condition=%wide.region_5.6_spmd.clone, body=%wide.region_4.5_spmd.clone.sunk | while | flops 262163 | bytes 2622325 | solution.py:88
  429.7 28.3 %all-reduce = f32[128]{0:T(128)S(1)} all-reduce(f32[128]{0:T(128)S(1)} %dynamic-update-slice), channel_id=2, replica_groups=mesh['seq'=16,'head'=16] {'seq'}, use_global_device_ids=true, to_apply=%add | all-reduce | flops 128 | bytes 1024
  458.1 22.3 %all-gather.4.cloned.1.call-done = f32[128,128,64]{1,2,0:T(8,128)} async-done(((f32[8,128,64]{1,2,0:T(8,128)}), f32[128,128,64]{1,2,0:T(8,128)}) %all-gather.4.cloned.1.call-update) | async-done | bytes 4194320 | tf_op jit(solution)/shard_map/all_gather | solution.py:12
  480.5 20.7 %while.44 = (s32[]{:T(128)}, f32[8,128,64]{2,1,0:T(8,128)S(1)}, s32[]{:T(128)}, f32[16,8]{1,0:T(8,128)S(1)}, f32[16,8,128,64]{2,3,1,0:T(8,128)}, /*index=5*/s32[]{:T(128)}, s32[]{:T(128)}, s32[]{:T(128)}) while((s32[]{:T(128)}, f32[8,128,64]{2,1,0:T(8,128)S(1)}, s32[]{:T(128)}, f32[16,8]{1,0:T(8,128)S(1)}, f32[16,8,128,64]{2,3,1,0:T(8,128)}, ...), condition=%wide.region_7.8_spmd, body=%wide.region_6.7_spmd.sunk | while | flops 131077 | bytes 1835231 | solution.py:20
  501.2 11.0 %fusion.27 = bf16[20,256,8,64]{1,3,2,0:T(8,128)(2,1)} fusion(f32[20,256,8,64]{1,3,2,0:T(8,128)} %get-tuple-element.133, f32[20,256,8]{1,2,0:T(8,128)S(1)} %exp.31, bf16[20,256,128,1]{2,1,3,0:T(8,128)(2,1)S(1)} %bitcast.152, f32[20,8,128,64]{3,2,1,0:T(8,128)} %get-tuple-element.136, f32[8,128,64]{2,1,0:T(8,128)S(1)} %get-tuple-element.140, f32[20,8]{1,0:T(8,128)S(1)} %exp.30), kind=kOutput, calls=%fused_computation.50 | convolution fusion | flops 682885120 | bytes 22708864 | tf_op jit(solution)/shard_map/cin,chnp->cihp/dot_general | solution.py:95
  512.2 10.9 %copy.77 = bf16[20,256,8,64]{3,2,1,0:T(8,128)(2,1)} copy(bf16[20,256,8,64]{1,3,2,0:T(8,128)(2,1)} %fusion.27) | data formatting | bytes 10485760 | tf_op jit(solution)/shard_map/reshape | solution.py:100
  523.1 14.6 %reshape.129 = bf16[16,320,512]{2,1,0:T(8,128)(2,1)} reshape(bf16[20,256,8,64]{3,2,1,0:T(8,128)(2,1)} %copy.77) | data formatting | bytes 10485760 | tf_op jit(solution)/shard_map/reshape | solution.py:100
  537.7 126.1 %all_to_all.75 = bf16[16,320,512]{2,1,0:T(8,128)(2,1)S(1)} all-to-all(bf16[16,320,512]{2,1,0:T(8,128)(2,1)} %reshape.129), channel_id=1, replica_groups=mesh['seq'=16,'head'=16] {'head'}, dimensions={0} | all-to-all | bytes 10485760 | tf_op jit(solution)/shard_map/all_to_all | solution.py:101
  663.9 3.1 copy.85
  (511 shorter events, 219.5 us)
Async XLA Ops:
  6.5 10.9 %copy-start = (bf16[320,1024]{1,0:T(8,128)(2,1)S(1)}, bf16[320,1024]{1,0:T(8,128)(2,1)}, u32[]{:S(2)}) copy-start(bf16[320,1024]{1,0:T(8,128)(2,1)} %param.13) | copy-start | bytes 1966084
  8.3 19.5 %all-to-all-start.3 = ((f32[320,16,8]{0,2,1:T(8,128)}), f32[320,16,8]{0,2,1:T(8,128)S(1)}, u32[]{:S(2)}, u32[]{:S(2)}) async-start(f32[320,16,8]{0,2,1:T(8,128)} %bitcast.25), calls=%async_computation.3 | async-start | bytes 393216 | tf_op jit(solution)/shard_map/all_to_all | solution.py:60
  29.1 36.4 %all-to-all-start.1 = ((bf16[320,16,128]{2,0,1:T(8,128)(2,1)}), bf16[320,16,128]{2,0,1:T(8,128)(2,1)S(1)}, u32[]{:S(2)}, u32[]{:S(2)}) async-start(bf16[320,16,128]{2,0,1:T(8,128)(2,1)} %bitcast.155), calls=%async_computation.1 | async-start | bytes 2621440 | tf_op jit(solution)/shard_map/all_to_all | solution.py:58
  65.5 4.6 copy-start.2
  65.5 120.1 %all-to-all-start = ((bf16[320,16,512]{2,0,1:T(8,128)(2,1)}), bf16[320,16,512]{2,0,1:T(8,128)(2,1)}, u32[]{:S(2)}, u32[]{:S(2)}) async-start(bf16[320,16,512]{2,0,1:T(8,128)(2,1)} %bitcast.149), calls=%async_computation | async-start | bytes 10485760 | tf_op jit(solution)/shard_map/all_to_all | solution.py:56
  186.9 38.8 %all-to-all-start.2 = ((bf16[320,16,128]{2,0,1:T(8,128)(2,1)}), bf16[320,16,128]{2,0,1:T(8,128)(2,1)}, u32[]{:S(2)}, u32[]{:S(2)}) async-start(bf16[320,16,128]{2,0,1:T(8,128)(2,1)} %bitcast.154), calls=%async_computation.2 | async-start | bytes 2621440 | tf_op jit(solution)/shard_map/all_to_all | solution.py:57
  192.4 288.0 %all-gather.4.cloned.1.call-start = ((), (), s32[]{:S(2)}) async-start(), calls=%async_computation.5 | async-start | bytes 4456448 | tf_op jit(solution)/shard_map/all_gather | solution.py:12
  382.8 45.3 %copy-start.3 = (u32[256]{0:T(256)S(1)}, u32[256]{0:T(256)}, u32[]{:S(2)}) copy-start(u32[256]{0:T(256)} %constant.71) | copy-start | bytes 3076
  663.9 3.1 copy-start.1
Sparse Core Ops, SparseCore 0:
  428.2 52.1 all-gather.3
where the time goes:
time: 680 us; the launch traced here: 674 us
  waiting for transfers between devices  183 us (27%)
  blocking collectives  154 us (23%)
  matrix products  123 us (18%)
  local copies, waits for them, and re-layouts  118 us (17%)
  other arithmetic  56.3 us (8%)
  starting transfers between devices  22.9 us (3%)
  between operations  14.2 us (2%)
    all_to_all x1, blocking collectives, shards(): lax.all_to_all(result, 'head', split_axis=0, concat_axis=2, tiled=True)  126 us
    all_to_all x1, waiting for transfers between devices, shards(): lax.all_to_all(features, 'head', split_axis=1, concat_axis=0, tiled=True)  115 us
    dot_general x20, matrix products, block_terms(): jnp.einsum('hij,jhp->ihp', weights, block_x, preferred_element_type=jnp.f...  48.1 us
    dot_general x20, matrix products, block_terms(): jnp.einsum('jhn,jhp->hnp', scaled, block_x, preferred_element_type=jnp.fl...  43.1 us
    unnamed x1, blocking collectives  28.3 us
    all_to_all x1, waiting for transfers between devices, shards(): lax.all_to_all(readers, 'head', split_axis=1, concat_axis=0, tiled=True)  27.3 us
    reshape x2, local copies, waits for them, and re-layouts, shards(): result = result.reshape(head_devices, local_rows, heads_dev * channels)  25.5 us
    dynamic_slice x40, local copies, waits for them, and re-layouts, shards(): lax.scan(advance, (empty_state, empty_decay), (span_ends, contribution))  23.4 us
  transfers between devices with their start and end apart: 5, of which 5 were waited for; matrix products, arithmetic and copies ran while one was open for 5% of the time, Pallas kernels for 0%

commit v1 on v0

v1 whole, which is shorter than its diff:
```python
import math

import jax
import jax.numpy as jnp
from jax import lax
from jax.experimental import pallas as pl
from jax.experimental.pallas import tpu as pltpu
from jax.sharding import Mesh, PartitionSpec as P

G = 8
LOG2E = math.log2(math.e)
VMEM_LIMIT = 16 * 1024 * 1024
EXTRA = 8
F32 = jnp.float32
BF16 = jnp.bfloat16


def split_two(a):
    high = a.astype(BF16)
    return high, (a - high.astype(F32)).astype(BF16)


def split_three(a):
    high = a.astype(BF16)
    rest = a - high.astype(F32)
    middle, low = split_two(rest)
    return high, middle, low


def head_columns(columns, channels, heads):
    row = lax.broadcasted_iota(jnp.int32, (heads, columns), 0)
    col = lax.broadcasted_iota(jnp.int32, (heads, columns), 1)
    shift = channels.bit_length() - 1
    pick = jnp.where(row == lax.shift_right_logical(col, shift), 1.0, 0.0).astype(BF16)
    return jnp.concatenate([pick, pick], axis=0)


def spread_heads(values, pick, base):
    values = pltpu.roll(values, values.shape[1] - base, axis=1)
    high, low = split_two(values)
    return jnp.dot(jnp.concatenate([high, low], axis=1), pick, preferred_element_type=F32)


def group_columns(ref, group, columns):
    return ref.at[:, pl.ds(pl.multiple_of(group * columns, columns), columns)]


def decay_rows(total, pick, base):
    heads = total.shape[1]
    total = pltpu.roll(jnp.broadcast_to(total, (EXTRA, heads)), heads - base, axis=1)
    high, middle, low = (part.astype(F32) for part in split_three(total))
    row = lax.broadcasted_iota(jnp.int32, (EXTRA, heads), 0)
    sides = []
    for start in (0, 3):
        rows = jnp.where(row == start, high, jnp.where(row == start + 1, middle, jnp.where(row == start + 2, low, 0.0)))
        sides.append(jnp.dot(rows.astype(BF16), pick[:heads], preferred_element_type=F32))
    return sides


def log_decays(rows):
    rows = rows.astype(F32)
    return tuple(rows[i + 2 : i + 3] + rows[i + 1 : i + 2] + rows[i : i + 1] for i in (0, 3))


def pack_decays(first, second):
    parts = [part.astype(F32) for whole in (first, second) for part in split_three(whole)]
    parts.append(jnp.zeros((EXTRA - len(parts), first.shape[1]), F32))
    return jnp.concatenate(parts, axis=0).astype(BF16)


def running_sum(a):
    length = a.shape[0]
    row = lax.broadcasted_iota(jnp.int32, (length, length), 0)
    col = lax.broadcasted_iota(jnp.int32, (length, length), 1)
    lower = jnp.where(row >= col, 1.0, 0.0).astype(BF16)
    high, middle, low = split_three(a)
    return (
        jnp.dot(lower, low, preferred_element_type=F32)
        + jnp.dot(lower, middle, preferred_element_type=F32)
        + jnp.dot(lower, high, preferred_element_type=F32)
    )


def write_group(channels, group, turn, x, writers, fade, total, pick, state_ref):
    columns = x.shape[1]
    base = group * (columns // channels)
    high, low = split_two(x.astype(F32) * spread_heads(fade, pick, base))
    state = lax.dot_general(
        jnp.concatenate([writers, writers], axis=0),
        jnp.concatenate([high, low], axis=0),
        (((0,), (0,)), ((), ())),
        preferred_element_type=F32,
    ).astype(BF16)
    decays = decay_rows(total, pick, base)
    blocks_n, blocks_c, rows, lanes = state_ref.shape
    rows = (rows - EXTRA) // 2
    count = columns // lanes // 2
    for j in range(count):
        left, middle, right = (k * lanes for k in (2 * j, 2 * j + 1, 2 * j + 2))
        extra = (decays[0][:, left:middle] + decays[1][:, middle:right]).astype(BF16)
        for i in range(blocks_n):
            span = slice(i * rows, (i + 1) * rows)
            state_ref[i, turn * count + j, :rows] = state[span, left:middle]
            state_ref[i, turn * count + j, rows : 2 * rows] = state[span, middle:right]
            state_ref[i, turn * count + j, 2 * rows :] = extra


def first_kernel(channels, side_ref, a_hbm, x_hbm, b_hbm, cum_ref, state_ref, x_ref, b_ref, fade_ref, pick_ref, a_sem, x_sems, b_sems):
    columns = x_ref.shape[1] // G
    state_size = b_ref.shape[1] // G
    half = G // 2
    length, heads = cum_ref.shape
    bring = pltpu.make_async_copy(a_hbm, cum_ref, a_sem)
    bring.start()
    copies = []
    for turn in range(G):
        side = side_ref[0] if turn < half else 1 - side_ref[0]
        group = side * half + turn % half
        pair = (
            pltpu.make_async_copy(
                group_columns(b_hbm, group, state_size), group_columns(b_ref, group, state_size), b_sems.at[turn]
            ),
            pltpu.make_async_copy(
                group_columns(x_hbm, group, columns), group_columns(x_ref, group, columns), x_sems.at[turn]
            ),
        )
        for copy in pair:
            copy.start()
        copies.append((group, pair))
    pick = head_columns(columns, channels, heads)
    bring.wait()
    cum = running_sum(cum_ref[...])
    cum_ref[...] = cum
    total = cum[length - 1 :, :]
    fade_ref[...] = jnp.exp(jnp.minimum(total - cum, 0.0))
    pick_ref[...] = pick
    for turn, (group, pair) in enumerate(copies):
        for copy in pair:
            copy.wait()
        if turn < half:
            write_group(
                channels, group, turn,
                group_columns(x_ref, group, columns)[...],
                group_columns(b_ref, group, state_size)[...],
                fade_ref[...], total, pick_ref[...], state_ref,
            )


def second_kernel(channels, side_ref, cum_ref, x_ref, b_ref, state_ref, fade_ref, pick_ref):
    columns = x_ref.shape[1] // G
    state_size = b_ref.shape[1] // G
    half = G // 2
    length, heads = cum_ref.shape
    cum = cum_ref[...]
    total = cum[length - 1 :, :]
    fade_ref[...] = jnp.exp(jnp.minimum(total - cum, 0.0))
    pick_ref[...] = head_columns(columns, channels, heads)
    for turn in range(half):
        group = side_ref[0] * half + turn
        write_group(
            channels, group, turn,
            group_columns(x_ref, group, columns)[...],
            group_columns(b_ref, group, state_size)[...],
            fade_ref[...], total, pick_ref[...], state_ref,
        )


WHOLE = pl.BlockSpec(memory_space=pltpu.VMEM)
SCALAR = pl.BlockSpec(memory_space=pltpu.SMEM)
LEFT = pl.BlockSpec(memory_space=pltpu.HBM)


def state_shape(length, width, state_size, pieces_n, pieces_c):
    lanes = width // 2 // pieces_c // 2
    return jax.ShapeDtypeStruct((pieces_n, pieces_c, 2 * state_size // pieces_n + EXTRA, lanes), BF16)


def first_states(side, log_decay, inputs, write_vectors, pieces_n, pieces_c):
    length, heads = log_decay.shape
    width = inputs.shape[1]
    return pl.pallas_call(
        lambda *refs: first_kernel(width // heads, *refs),
        in_specs=[SCALAR, LEFT, LEFT, LEFT],
        out_specs=[WHOLE] * 4,
        out_shape=[
            jax.ShapeDtypeStruct(log_decay.shape, F32),
            state_shape(length, width, write_vectors.shape[1] // G, pieces_n, pieces_c),
            jax.ShapeDtypeStruct(inputs.shape, BF16),
            jax.ShapeDtypeStruct(write_vectors.shape, BF16),
        ],
        scratch_shapes=[
            pltpu.VMEM((length, heads), F32),
            pltpu.VMEM((2 * heads, width // G), BF16),
            pltpu.SemaphoreType.DMA,
            pltpu.SemaphoreType.DMA((G,)),
            pltpu.SemaphoreType.DMA((G,)),
        ],
        compiler_params=pltpu.CompilerParams(vmem_limit_bytes=VMEM_LIMIT),
        cost_estimate=pl.CostEstimate(flops=2 * length * 256 * width, bytes_accessed=4 * inputs.size, transcendentals=0),
    )(side, *(pltpu.with_memory_space_constraint(a, pltpu.HBM) for a in (log_decay, inputs, write_vectors)))


def second_states(side, cumulative, inputs, write_vectors, pieces_n, pieces_c):
    length, heads = cumulative.shape
    width = inputs.shape[1]
    return pl.pallas_call(
        lambda *refs: second_kernel(width // heads, *refs),
        in_specs=[SCALAR, WHOLE, WHOLE, WHOLE],
        out_specs=WHOLE,
        out_shape=state_shape(length, width, write_vectors.shape[1] // G, pieces_n, pieces_c),
        scratch_shapes=[pltpu.VMEM((length, heads), F32), pltpu.VMEM((2 * heads, width // G), BF16)],
        compiler_params=pltpu.CompilerParams(vmem_limit_bytes=VMEM_LIMIT),
        cost_estimate=pl.CostEstimate(flops=2 * length * 256 * width, bytes_accessed=inputs.size, transcendentals=0),
    )(side, cumulative, inputs, write_vectors)


def join_kernel(side_ref, kept_ref, came_ref, out_ref):
    blocks_n, blocks_c, rows, _ = kept_ref.shape
    rows = (rows - EXTRA) // 2

    def join(first_ref, second_ref):
        for j in range(blocks_c):
            before = log_decays(first_ref[0, j, 2 * rows :])
            after = log_decays(second_ref[0, j, 2 * rows :])
            extra = pack_decays(*(a + b for a, b in zip(before, after)))
            for k in range(2):
                span = slice(k * rows, (k + 1) * rows)
                decay = jnp.exp(after[k])
                for i in range(blocks_n):
                    out_ref[i, j, span] = (
                        decay * first_ref[i, j, span].astype(F32) + second_ref[i, j, span].astype(F32)
                    ).astype(BF16)
            for i in range(blocks_n):
                out_ref[i, j, 2 * rows :] = extra

    @pl.when(side_ref[0] == 0)
    def _():
        join(kept_ref, came_ref)

    @pl.when(side_ref[0] == 1)
    def _():
        join(came_ref, kept_ref)


def on_chip(kernel, shape, side, *arrays):
    whole = pl.BlockSpec(memory_space=pltpu.VMEM)
    return pl.pallas_call(
        kernel,
        in_specs=[pl.BlockSpec(memory_space=pltpu.SMEM)] + [whole] * len(arrays),
        out_specs=whole,
        out_shape=jax.ShapeDtypeStruct(shape, BF16),
        compiler_params=pltpu.CompilerParams(vmem_limit_bytes=VMEM_LIMIT),
    )(side, *arrays)


def joined(side, kept, came):
    return on_chip(join_kernel, kept.shape, side, kept, came)


def give_kernel(side_ref, held_ref, kept_ref, out_ref):
    blocks_n, blocks_c, rows, _ = held_ref.shape
    rows = rows // 2

    @pl.when(side_ref[0] == 0)
    def _():
        for j in range(blocks_c):
            logs = log_decays(kept_ref[0, j, 2 * rows :])
            for k in range(2):
                span = slice(k * rows, (k + 1) * rows)
                decay = jnp.exp(logs[k])
                for i in range(blocks_n):
                    out_ref[i, j, span] = (
                        decay * held_ref[i, j, span].astype(F32) + kept_ref[i, j, span].astype(F32)
                    ).astype(BF16)

    @pl.when(side_ref[0] == 1)
    def _():
        out_ref[...] = held_ref[...]


def given(side, held, kept):
    return on_chip(give_kernel, held.shape, side, held, kept)


def diagonal_kernel(channels, side_ref, cum_ref, x_ref, b_ref, c_ref, out_ref, cum_rows, cum_cols, scores):
    length, heads = cum_ref.shape
    columns = x_ref.shape[1] // G
    state_size = b_ref.shape[1] // G
    per_group = columns // channels
    half = G // 2
    padded = cum_rows.shape[1]

    scaled = cum_ref[...] * LOG2E
    cum_cols[...] = scaled
    tall = jnp.concatenate([scaled, jnp.zeros((padded - length, heads), F32)], axis=0)
    cum_rows[...] = tall.T

    def one(turn, _):
        group = turn + side_ref[0] * half
        diagonal_group(
            channels, group, cum_rows, cum_cols, scores,
            group_columns(x_ref, group, columns),
            group_columns(b_ref, group, state_size)[...],
            group_columns(c_ref, group, state_size)[...],
            group_columns(out_ref, turn, columns),
        )
        return 0

    lax.fori_loop(0, half, one, 0)


def diagonal_group(channels, group, cum_rows, cum_cols, scores, x_ref, writers, readers, out_ref):
    length, heads = cum_cols.shape
    per_group = x_ref.shape[1] // channels
    tile = 128
    sc = lax.dot_general(
        readers, writers, (((1,), (1,)), ((), ())), preferred_element_type=F32
    )
    row = lax.broadcasted_iota(jnp.int32, (length, length), 0)
    col = lax.broadcasted_iota(jnp.int32, (length, length), 1)
    scores[...] = jnp.where(row >= col, sc, 0.0)

    base = pl.multiple_of(group * per_group, per_group)
    rows_all = cum_rows[pl.ds(base, per_group), :]
    cols_all = pltpu.roll(cum_cols[...], heads - base, axis=1)
    starts = list(range(0, length, tile))

    def weights(head, top, bottom):
        column = cols_all[top:bottom, head : head + 1]
        parts = []
        for left in range(0, bottom, tile):
            right = min(left + tile, bottom)
            gap = column - rows_all[head : head + 1, left:right]
            if right > top:
                gap = jnp.minimum(gap, 0.0)
            parts.append((jnp.exp2(gap) * scores[top:bottom, left:right]).astype(BF16))
        return parts[0] if len(parts) == 1 else jnp.concatenate(parts, axis=1)

    lane = lax.broadcasted_iota(jnp.int32, (1, 2 * channels), 1)
    for pair in range(per_group // 2):
        x_pair = x_ref[:, pair * 2 * channels : (pair + 1) * 2 * channels]
        for top in starts:
            bottom = min(top + tile, length)
            both = jnp.concatenate(
                [weights(2 * pair, top, bottom), weights(2 * pair + 1, top, bottom)], axis=0
            )
            mixed = jnp.dot(both, x_pair[:bottom], preferred_element_type=F32)
            out_ref[top:bottom, pair * 2 * channels : (pair + 1) * 2 * channels] = jnp.where(
                lane < channels, mixed[: bottom - top], mixed[bottom - top :]
            )


def diagonals(side, cumulative, inputs, write_vectors, read_vectors):
    length, heads = cumulative.shape
    width = inputs.shape[1]
    padded = -(-length // 128) * 128
    return pl.pallas_call(
        lambda *refs: diagonal_kernel(width // heads, *refs),
        in_specs=[SCALAR] + [WHOLE] * 4,
        out_specs=WHOLE,
        out_shape=jax.ShapeDtypeStruct((length, width // 2), F32),
        scratch_shapes=[
            pltpu.VMEM((heads, padded), F32),
            pltpu.VMEM((length, heads), F32),
            pltpu.VMEM((length, length), F32),
        ],
        compiler_params=pltpu.CompilerParams(vmem_limit_bytes=VMEM_LIMIT),
        cost_estimate=pl.CostEstimate(
            flops=length * length * width,
            bytes_accessed=3 * length * width,
            transcendentals=length * length * heads // 2,
        ),
    )(side, cumulative, inputs, write_vectors, read_vectors)


def scan_kernel(side_ref, term_ref, out_ref):
    chips, rows, lanes = out_ref.shape
    rows = rows // 2
    block = 8

    def some(i, states):
        for k in range(block):
            at = i * block + k
            decays = log_decays(term_ref[at, 2 * rows :])
            after = []
            for side in range(2):
                span = slice(side * rows, (side + 1) * rows)
                out_ref[at, span] = states[side].astype(BF16)
                after.append(jnp.exp(decays[side]) * states[side] + term_ref[at, span].astype(F32))
            states = tuple(after)
        return states

    lax.fori_loop(0, chips // block, some, (jnp.zeros((rows, lanes), F32),) * 2)


def entries(side, terms):
    chips, rows, lanes = terms.shape
    return on_chip(scan_kernel, (chips, rows - EXTRA, lanes), side, terms)


def read_kernel(channels, mine, side_ref, cum_ref, c_ref, diagonal_ref, held_ref, *rest):
    out_hbm, grown_ref, pick_ref, out_ref, sems = rest[-5:]
    half, _, columns = out_ref.shape
    state_size = c_ref.shape[1] // G
    grown_ref[...] = jnp.exp(cum_ref[...])
    pick_ref[...] = head_columns(columns, channels, cum_ref.shape[1])
    blocks_n, blocks_c, rows, lanes = held_ref.shape
    rows = rows // 2
    count = blocks_c // half
    copies = []
    for turn in range(half):
        group = side_ref[0] * half + turn
        decay = spread_heads(grown_ref[...], pick_ref[...], group * (columns // channels))
        readers = group_columns(c_ref, group, state_size)[...]
        if mine:
            readers = jnp.concatenate([readers, readers], axis=1)
        for j in range(count):
            sides = []
            for k in range(2):
                at = turn * count + j
                span = slice(k * rows, (k + 1) * rows)
                held = jnp.concatenate([held_ref[i, at, span] for i in range(blocks_n)], axis=0)
                if mine:
                    came_ref = rest[0]
                    second = side_ref[0] == 1
                    came = jnp.concatenate([came_ref[i, at, span] for i in range(blocks_n)], axis=0)
                    logs = log_decays(came_ref[0, at, 2 * rows :])[k]
                    scale = jnp.exp(jnp.where(second, logs, 0.0))
                    start = scale * held.astype(F32) + jnp.where(second, came.astype(F32), 0.0)
                    held = jnp.concatenate(split_two(start), axis=0)
                sides.append(held)
            read = jnp.dot(readers, jnp.concatenate(sides, axis=1), preferred_element_type=F32)
            span = slice(2 * j * lanes, (2 * j + 2) * lanes)
            wide = slice(turn * columns + 2 * j * lanes, turn * columns + (2 * j + 2) * lanes)
            out_ref[turn, :, span] = (diagonal_ref[:, wide] + read * decay[:, span]).astype(BF16)
        copy = pltpu.make_async_copy(out_ref.at[turn], group_columns(out_hbm, group, columns), sems.at[turn])
        copy.start()
        copies.append(copy)
    for copy in copies:
        copy.wait()


def outputs(side, cumulative, read_vectors, diagonal, held, came=None, done=None):
    length, heads = cumulative.shape
    half = G // 2
    width = diagonal.shape[1] * 2
    columns = width // G
    in_specs = [SCALAR] + [WHOLE] * 4
    args = [side, cumulative, read_vectors, diagonal, held]
    aliases = {}
    if came is not None:
        in_specs.append(WHOLE)
        args.append(came)
    if done is not None:
        in_specs.append(LEFT)
        aliases = {len(args): 0}
        args.append(done)
    return pl.pallas_call(
        lambda *refs: read_kernel(width // heads, came is not None, *refs),
        in_specs=in_specs,
        out_specs=LEFT,
        scratch_shapes=[
            pltpu.VMEM((length, heads), F32),
            pltpu.VMEM((2 * heads, columns), BF16),
            pltpu.VMEM((half, length, columns), BF16),
            pltpu.SemaphoreType.DMA((half,)),
        ],
        out_shape=jax.ShapeDtypeStruct((length, width), BF16),
        input_output_aliases=aliases,
        compiler_params=pltpu.CompilerParams(vmem_limit_bytes=VMEM_LIMIT),
        cost_estimate=pl.CostEstimate(
            flops=2 * length * 128 * width,
            bytes_accessed=2 * length * width,
            transcendentals=0,
        ),
    )(*args)


def shards(inputs, log_decay, write_vectors, read_vectors):
    chips = lax.axis_size("seq") * lax.axis_size("z")
    pieces_n = 8
    pieces_c = chips // pieces_n
    own_side = lax.axis_index("c").astype(jnp.int32).reshape(1)
    other_side = 1 - own_side
    swap = [(0, 1), (1, 0)]

    cumulative, gone, inputs, write_vectors = first_states(
        other_side, log_decay, inputs, write_vectors, pieces_n, pieces_c
    )
    came = lax.ppermute(gone, "c", swap)
    kept = second_states(own_side, cumulative, inputs, write_vectors, pieces_n, pieces_c)
    term = joined(own_side, kept, came)

    terms = lax.all_to_all(term.reshape((chips,) + term.shape[2:]), ("seq", "z"), 0, 0, tiled=True)
    diagonal_own = diagonals(own_side, cumulative, inputs, write_vectors, read_vectors)
    terms, diagonal_own = lax.optimization_barrier((terms, diagonal_own))

    held = lax.all_to_all(entries(own_side, terms), ("seq", "z"), 0, 0, tiled=True)
    diagonal_other = diagonals(other_side, cumulative, inputs, write_vectors, read_vectors)
    held, diagonal_other = lax.optimization_barrier((held, diagonal_other))
    held = held.reshape(term.shape[:2] + held.shape[1:])

    held_other = lax.ppermute(given(own_side, held, kept), "c", swap)
    done = outputs(own_side, cumulative, read_vectors, diagonal_own, held, came=came)
    return outputs(other_side, cumulative, read_vectors, diagonal_other, held_other, done=done)


def solution(mesh):
    seq, head = mesh.devices.shape
    fine = Mesh(mesh.devices.reshape(seq, head // 2, 2), ("seq", "z", "c"))
    spec = P(("seq", "z", "c"), None)
    return jax.shard_map(
        shards, mesh=fine, in_specs=(spec,) * 4, out_specs=spec, check_vma=False
    )
```

time: 680 us -> 115 us (0.17)
  the two profiles are of different devices: /device:TPU:31 before, /device:TPU:1 now
where the time goes in v1:
time: 115 us; the launch traced here: 114 us
  waiting for transfers between devices  44.1 us (38%)
  starting transfers between devices  27.8 us (24%)
  Pallas kernels  23.9 us (21%)
  local copies, waits for them, and re-layouts  18.3 us (16%)
    all_to_all x1, waiting for transfers between devices, shards(): lax.all_to_all(term.reshape((chips,) + term.shape[2:]), ('seq', 'z'), 0,...  25.7 us
    unnamed x32, local copies, waits for them, and re-layouts  18.3 us
    all_to_all x1, waiting for transfers between devices, shards(): lax.all_to_all(entries(own_side, terms), ('seq', 'z'), 0, 0, tiled=True)  18.1 us
    all_to_all x1, starting transfers between devices, shards(): lax.all_to_all(term.reshape((chips,) + term.shape[2:]), ('seq', 'z'), 0,...  13.8 us
    pallas_call x2, Pallas kernels, diagonals(): pl.pallas_call(lambda *refs: diagonal_kernel(width // heads, *refs), in_s...  9.54 us
    all_to_all x1, starting transfers between devices, shards(): lax.all_to_all(entries(own_side, terms), ('seq', 'z'), 0, 0, tiled=True)  6.37 us
    pallas_call x1, Pallas kernels, first_states(): pl.pallas_call(lambda *refs: first_kernel(width // heads, *refs), in_spec...  5.95 us
    pallas_call x2, Pallas kernels, outputs(): pl.pallas_call(lambda *refs: read_kernel(width // heads, came is not None...  4.98 us
  transfers between devices with their start and end apart: 4, of which 3 were waited for; matrix products, arithmetic and copies ran while one was open for 0% of the time, Pallas kernels for 13%

profile of v1, /device:TPU:1, one launch (start us, length us, event | category | flops | bytes accessed | tf_op | source)
XLA Modules:
  0.0 114.5 jit_solution(11961445938599959907)
XLA Ops:
  0.0 5.9 %shard_map.46 = (f32[320,128]{1,0:T(8,128)S(1)}, bf16[8,16,40,128]{3,2,1,0:T(8,128)(2,1)S(1)}, bf16[320,8192]{1,0:T(8,128)(2,1)S(1)}, bf16[320,1024]{1,0:T(8,128)(2,1)S(1)}) custom-call(s32[1]{0:T(128)S(6)} %sub.3.refs_0_, f32[320,128]{1,0:T(8,128)} %refs_1_.1, bf16[320,8192]{1,0:T(8,128)(2,1)} %refs_2_.3, bf16[320,1024]{1,0:T(8,128)(2,1)} %refs_3_.1), custom_call_target="tpu_custom_call" | custom-call | flops 1342177280 | bytes 10485760 | tf_op jit(solution)/shard_map/pallas_call | solution.py:181
  6.0 3.3 %collective-permute-start = (bf16[8,16,40,128]{3,2,1,0:T(8,128)(2,1)S(1)}, bf16[8,16,40,128]{3,2,1,0:T(8,128)(2,1)S(1)}, u32[]{:S(2)}, u32[]{:S(2)}) collective-permute-start(bf16[8,16,40,128]{3,2,1,0:T(8,128)(2,1)S(1)} %get-tuple-element.16), channel_id=1, source_target_pairs={{0,1},{1,0},{2,3},{3,2},{4,5},{5,4},{6,7},{7,6},{8,9},{9,8},{10,11... | collective-permute-start | bytes 3932168 | tf_op jit(solution)/shard_map/ppermute | solution.py:490
  9.3 2.3 %shard_map.47.kept_ref = bf16[8,16,40,128]{3,2,1,0:T(8,128)(2,1)S(1)} custom-call(s32[1]{0:T(128)} %bitcast.refs_0_.side_ref, f32[320,128]{1,0:T(8,128)S(1)} %get-tuple-element.13.refs_1_, bf16[320,8192]{1,0:T(8,128)(2,1)S(1)} %get-tuple-element.14.refs_2_, bf16[320,1024]{1,0:T(8,128)(2,1)S(1)} %get-tuple-element.15.refs_3_), custom_call_target="tpu_custom_call" | custom-call | flops 1342177280 | bytes 2621440 | tf_op jit(solution)/shard_map/pallas_call | solution.py:206
  12.0 0.5 shard_map.48
  12.5 0.5 copy-done.7
  13.0 1.1 copy-done.3
  14.1 13.8 %all-to-all-start = ((bf16[128,40,128]{2,1,0:T(8,128)(2,1)}), bf16[128,40,128]{2,1,0:T(8,128)(2,1)S(1)}, u32[]{:S(2)}, u32[]{:S(2)}) async-start(bf16[128,40,128]{2,1,0:T(8,128)(2,1)} %bitcast.7), calls=%async_computation | async-start | bytes 2621440 | tf_op jit(solution)/shard_map/all_to_all | solution.py:494
  27.9 2.5 %copy-done.5 = bf16[320,8192]{1,0:T(8,128)(2,1)S(1)} copy-done((bf16[320,8192]{1,0:T(8,128)(2,1)S(1)}, bf16[320,8192]{1,0:T(8,128)(2,1)}, u32[]{:S(2)}) %copy-start.5) | copy-done | bytes 5242904
  30.4 1.1 copy-done.12
  31.5 4.8 %shard_map.49.refs_3_ = f32[320,4096]{1,0:T(8,128)S(1)} custom-call(s32[1]{0:T(128)} %bitcast.refs_0_.side_ref, f32[320,128]{1,0:T(8,128)S(1)} %get-tuple-element.13.refs_1_, bf16[320,8192]{1,0:T(8,128)(2,1)S(1)} %copy-done.5, bf16[320,1024]{1,0:T(8,128)(2,1)S(1)} %copy-done.12, bf16[320,1024]{1,0:T(8,128)(2,1)S(1)} %copy-done.10), custom_call_target="tpu_custom_call" | custom-call | flops 838860800 | bytes 7864320 | tf_op jit(solution)/shard_map/pallas_call | solution.py:357
  36.3 2.3 %copy-done.1 = f32[320,4096]{1,0:T(8,128)} copy-done((f32[320,4096]{1,0:T(8,128)}, f32[320,4096]{1,0:T(8,128)S(1)}, u32[]{:S(2)}) %copy-start.1) | copy-done | bytes 5242904
  38.6 25.7 %all-to-all-done.term_ref = bf16[128,40,128]{2,1,0:T(8,128)(2,1)S(1)} async-done(((bf16[128,40,128]{2,1,0:T(8,128)(2,1)}), bf16[128,40,128]{2,1,0:T(8,128)(2,1)S(1)}, u32[]{:S(2)}, u32[]{:S(2)}) %all-to-all-start) | async-done | bytes 1310752 | tf_op jit(solution)/shard_map/all_to_all | solution.py:494
  64.9 1.0 copy-done.9
  65.9 6.4 %all-to-all-start.1 = ((bf16[128,32,128]{2,1,0:T(8,128)(2,1)}), bf16[128,32,128]{2,1,0:T(8,128)(2,1)S(1)}, u32[]{:S(2)}, u32[]{:S(2)}) async-start(bf16[128,32,128]{2,1,0:T(8,128)(2,1)} %copy-done.9), calls=%async_computation.1 | async-start | bytes 2097152 | tf_op jit(solution)/shard_map/all_to_all | solution.py:498
  72.2 2.5 %copy-done.6 = bf16[320,8192]{1,0:T(8,128)(2,1)S(1)} copy-done((bf16[320,8192]{1,0:T(8,128)(2,1)S(1)}, bf16[320,8192]{1,0:T(8,128)(2,1)}, u32[]{:S(2)}) %copy-start.6) | copy-done | bytes 5242904
  74.7 1.1 copy-done.13
  75.8 4.8 %shard_map.51.refs_3_ = f32[320,4096]{1,0:T(8,128)S(1)} custom-call(s32[1]{0:T(128)S(6)} %sub.3.refs_0_, f32[320,128]{1,0:T(8,128)S(1)} %get-tuple-element.13.refs_1_, bf16[320,8192]{1,0:T(8,128)(2,1)S(1)} %copy-done.6, bf16[320,1024]{1,0:T(8,128)(2,1)S(1)} %copy-done.13, bf16[320,1024]{1,0:T(8,128)(2,1)S(1)} %copy-done.10), custom_call_target="tpu_custom_call" | custom-call | flops 838860800 | bytes 7864320 | tf_op jit(solution)/shard_map/pallas_call | solution.py:357
  80.6 2.4 %copy-done = f32[320,4096]{1,0:T(8,128)} copy-done((f32[320,4096]{1,0:T(8,128)}, f32[320,4096]{1,0:T(8,128)S(1)}, u32[]{:S(2)}) %copy-start) | copy-done | bytes 5242904
  83.0 18.1 %all-to-all-done.1 = bf16[128,32,128]{2,1,0:T(8,128)(2,1)S(1)} async-done(((bf16[128,32,128]{2,1,0:T(8,128)(2,1)}), bf16[128,32,128]{2,1,0:T(8,128)(2,1)S(1)}, u32[]{:S(2)}, u32[]{:S(2)}) %all-to-all-start.1) | async-done | bytes 1048608 | tf_op jit(solution)/shard_map/all_to_all | solution.py:498
  101.1 4.3 %collective-permute-start.1 = (bf16[8,16,32,128]{3,2,1,0:T(8,128)(2,1)S(1)}, bf16[8,16,32,128]{3,2,1,0:T(8,128)(2,1)S(1)}, u32[]{:S(2)}, u32[]{:S(2)}) collective-permute-start(bf16[8,16,32,128]{3,2,1,0:T(8,128)(2,1)S(1)} %shard_map.52), channel_id=1, source_target_pairs={{0,1},{1,0},{2,3},{3,2},{4,5},{5,4},{6,7},{7,6},{8,9},{9,8},{10,11... | collective-permute-start | bytes 3145736 | tf_op jit(solution)/shard_map/ppermute | solution.py:503
  105.5 2.5 %copy-done.2 = f32[320,4096]{1,0:T(8,128)S(1)} copy-done((f32[320,4096]{1,0:T(8,128)S(1)}, f32[320,4096]{1,0:T(8,128)}, u32[]{:S(2)}) %copy-start.2) | copy-done | bytes 5242904
  108.0 1.3 %copy-done.8 = bf16[8,16,40,128]{3,2,1,0:T(8,128)(2,1)S(1)} copy-done((bf16[8,16,40,128]{3,2,1,0:T(8,128)(2,1)S(1)}, bf16[8,16,40,128]{3,2,1,0:T(8,128)(2,1)}, u32[]{:S(2)}) %copy-start.8) | copy-done | bytes 1310744
  109.3 2.5 %shard_map.53.refs_5_ = bf16[320,8192]{1,0:T(8,128)(2,1)} custom-call(s32[1]{0:T(128)} %bitcast.refs_0_.side_ref, f32[320,128]{1,0:T(8,128)S(1)} %get-tuple-element.13.refs_1_, bf16[320,1024]{1,0:T(8,128)(2,1)S(1)} %copy-done.10, f32[320,4096]{1,0:T(8,128)S(1)} %copy-done.2, bf16[8,16,32,128]{3,2,1,0:T(8,128)(2,1)S(1)} %bitcast.4, ...), custom_call_target="tpu_custom_call" | custom-call | flops 671088640 | bytes 5242880 | tf_op jit(solution)/shard_map/pallas_call | solution.py:458
  111.8 2.5 %shard_map.54 = bf16[320,8192]{1,0:T(8,128)(2,1)} custom-call(s32[1]{0:T(128)S(6)} %sub.3.refs_0_, f32[320,128]{1,0:T(8,128)S(1)} %get-tuple-element.13.refs_1_, bf16[320,1024]{1,0:T(8,128)(2,1)S(1)} %copy-done.10, f32[320,4096]{1,0:T(8,128)S(1)} %bitcast.6, ...), custom_call_target="tpu_custom_call", output_to_operand_aliasing={{}: (5, {})} | custom-call | flops 671088640 | bytes 5242880 | tf_op jit(solution)/shard_map/pallas_call | solution.py:458
  (26 shorter events, 0.9 us)
Async XLA Ops:
  6.0 5.7 %copy-start.4 = (bf16[320,8192]{1,0:T(8,128)(2,1)}, bf16[320,8192]{1,0:T(8,128)(2,1)S(1)}, u32[]{:S(2)}) copy-start(bf16[320,8192]{1,0:T(8,128)(2,1)S(1)} %get-tuple-element.14.refs_2_) | copy-start | bytes 15728644
  6.0 6.5 %copy-start.11 = (bf16[320,1024]{1,0:T(8,128)(2,1)}, bf16[320,1024]{1,0:T(8,128)(2,1)S(1)}, u32[]{:S(2)}) copy-start(bf16[320,1024]{1,0:T(8,128)(2,1)S(1)} %get-tuple-element.15.refs_3_) | copy-start | bytes 1966084
  6.0 6.0 %collective-permute-start = (bf16[8,16,40,128]{3,2,1,0:T(8,128)(2,1)S(1)}, bf16[8,16,40,128]{3,2,1,0:T(8,128)(2,1)S(1)}, u32[]{:S(2)}, u32[]{:S(2)}) collective-permute-start(bf16[8,16,40,128]{3,2,1,0:T(8,128)(2,1)S(1)} %get-tuple-element.16), channel_id=1, source_target_pairs={{0,1},{1,0},{2,3},{3,2},{4,5},{5,4},{6,7},{7,6},{8,9},{9,8},{10,11... | collective-permute-start | bytes 3932168 | tf_op jit(solution)/shard_map/ppermute | solution.py:490
  9.3 18.6 %copy-start.10 = (bf16[320,1024]{1,0:T(8,128)(2,1)S(1)}, bf16[320,1024]{1,0:T(8,128)(2,1)}, u32[]{:S(2)}) copy-start(bf16[320,1024]{1,0:T(8,128)(2,1)} %refs_2_.5) | copy-start | bytes 1966084
  12.0 1.1 copy-start.7
  13.0 1.1 copy-start.3
  14.1 50.2 %all-to-all-start = ((bf16[128,40,128]{2,1,0:T(8,128)(2,1)}), bf16[128,40,128]{2,1,0:T(8,128)(2,1)S(1)}, u32[]{:S(2)}, u32[]{:S(2)}) async-start(bf16[128,40,128]{2,1,0:T(8,128)(2,1)} %bitcast.7), calls=%async_computation | async-start | bytes 2621440 | tf_op jit(solution)/shard_map/all_to_all | solution.py:494
  27.9 2.5 %copy-start.5 = (bf16[320,8192]{1,0:T(8,128)(2,1)S(1)}, bf16[320,8192]{1,0:T(8,128)(2,1)}, u32[]{:S(2)}) copy-start(bf16[320,8192]{1,0:T(8,128)(2,1)} %copy-done.4) | copy-start | bytes 15728644
  30.4 1.1 copy-start.12
  36.3 2.4 %copy-start.1 = (f32[320,4096]{1,0:T(8,128)}, f32[320,4096]{1,0:T(8,128)S(1)}, u32[]{:S(2)}) copy-start(f32[320,4096]{1,0:T(8,128)S(1)} %shard_map.49.refs_3_) | copy-start | bytes 15728644
  64.8 1.0 copy-start.9
  65.9 35.2 %all-to-all-start.1 = ((bf16[128,32,128]{2,1,0:T(8,128)(2,1)}), bf16[128,32,128]{2,1,0:T(8,128)(2,1)S(1)}, u32[]{:S(2)}, u32[]{:S(2)}) async-start(bf16[128,32,128]{2,1,0:T(8,128)(2,1)} %copy-done.9), calls=%async_computation.1 | async-start | bytes 2097152 | tf_op jit(solution)/shard_map/all_to_all | solution.py:498
  72.2 2.5 %copy-start.6 = (bf16[320,8192]{1,0:T(8,128)(2,1)S(1)}, bf16[320,8192]{1,0:T(8,128)(2,1)}, u32[]{:S(2)}) copy-start(bf16[320,8192]{1,0:T(8,128)(2,1)} %copy-done.4) | copy-start | bytes 15728644
  74.7 1.1 copy-start.13
  80.6 2.4 %copy-start = (f32[320,4096]{1,0:T(8,128)}, f32[320,4096]{1,0:T(8,128)S(1)}, u32[]{:S(2)}) copy-start(f32[320,4096]{1,0:T(8,128)S(1)} %shard_map.51.refs_3_) | copy-start | bytes 15728644
  101.1 10.7 %slice-start = ((s8[5242880]{0:T(1024)(128)(4,1)}), s8[4194304]{0:T(1024)(128)(4,1)S(1)}, s32[]{:S(2)}) async-start(s8[5242880]{0:T(1024)(128)(4,1)} %bitcast.5), calls=%async_computation.2 | async-start | bytes 8388608
  101.1 10.7 %slice-start.1 = ((s8[5242880]{0:T(1024)(128)(4,1)}), s8[1048576]{0:T(1024)(128)(4,1)S(1)}, s32[]{:S(2)}) async-start(s8[5242880]{0:T(1024)(128)(4,1)} %bitcast.5), calls=%async_computation.3 | async-start | bytes 2097152
  101.1 10.6 %collective-permute-start.1 = (bf16[8,16,32,128]{3,2,1,0:T(8,128)(2,1)S(1)}, bf16[8,16,32,128]{3,2,1,0:T(8,128)(2,1)S(1)}, u32[]{:S(2)}, u32[]{:S(2)}) collective-permute-start(bf16[8,16,32,128]{3,2,1,0:T(8,128)(2,1)S(1)} %shard_map.52), channel_id=1, source_target_pairs={{0,1},{1,0},{2,3},{3,2},{4,5},{5,4},{6,7},{7,6},{8,9},{9,8},{10,11... | collective-permute-start | bytes 3145736 | tf_op jit(solution)/shard_map/ppermute | solution.py:503
  105.5 2.5 %copy-start.2 = (f32[320,4096]{1,0:T(8,128)S(1)}, f32[320,4096]{1,0:T(8,128)}, u32[]{:S(2)}) copy-start(f32[320,4096]{1,0:T(8,128)} %copy-done.1) | copy-start | bytes 15728644
  108.0 1.3 %copy-start.8 = (bf16[8,16,40,128]{3,2,1,0:T(8,128)(2,1)S(1)}, bf16[8,16,40,128]{3,2,1,0:T(8,128)(2,1)}, u32[]{:S(2)}) copy-start(bf16[8,16,40,128]{3,2,1,0:T(8,128)(2,1)} %copy-done.7) | copy-start | bytes 3932164

commit v2 on v1

--- a/solution.py
+++ b/solution.py
@@ -1,3 +1,4 @@
+import functools
 import math
 
 import jax
@@ -214,7 +215,7 @@
     )(side, cumulative, inputs, write_vectors)
 
 
-def join_kernel(side_ref, kept_ref, came_ref, out_ref):
+def join_kernel(parts, side_ref, kept_ref, came_ref, out_hbm, out_ref, sems):
     blocks_n, blocks_c, rows, _ = kept_ref.shape
     rows = (rows - EXTRA) // 2
 
@@ -232,6 +233,8 @@
                     ).astype(BF16)
             for i in range(blocks_n):
                 out_ref[i, j, 2 * rows :] = extra
+            if (j + 1) % (blocks_c // parts) == 0:
+                part_copy(parts, j * parts // blocks_c, out_ref, out_hbm, sems).start()
 
     @pl.when(side_ref[0] == 0)
     def _():
@@ -240,6 +243,9 @@
     @pl.when(side_ref[0] == 1)
     def _():
         join(came_ref, kept_ref)
+
+    for part in range(parts):
+        part_copy(parts, part, out_ref, out_hbm, sems).wait()
 
 
 def on_chip(kernel, shape, side, *arrays):
@@ -253,8 +259,27 @@
     )(side, *arrays)
 
 
+def off_chip(kernel, shape, side, *arrays):
+    parts = 4
+    whole = pl.BlockSpec(memory_space=pltpu.VMEM)
+    return pl.pallas_call(
+        functools.partial(kernel, parts),
+        in_specs=[pl.BlockSpec(memory_space=pltpu.SMEM)] + [whole] * len(arrays),
+        out_specs=LEFT,
+        out_shape=pltpu.HBM(shape, BF16),
+        scratch_shapes=[pltpu.VMEM(shape, BF16), pltpu.SemaphoreType.DMA((parts,))],
+        compiler_params=pltpu.CompilerParams(vmem_limit_bytes=VMEM_LIMIT),
+    )(side, *arrays)
+
+
+def part_copy(parts, part, out_ref, out_hbm, sems):
+    size = out_ref.shape[1] // parts
+    span = pl.ds(part * size, size)
+    return pltpu.make_async_copy(out_ref.at[:, span], out_hbm.at[:, span], sems.at[part])
+
+
 def joined(side, kept, came):
-    return on_chip(join_kernel, kept.shape, side, kept, came)
+    return off_chip(join_kernel, kept.shape, side, kept, came)
 
 
 def give_kernel(side_ref, held_ref, kept_ref, out_ref):
@@ -373,29 +398,33 @@
     )(side, cumulative, inputs, write_vectors, read_vectors)
 
 
-def scan_kernel(side_ref, term_ref, out_ref):
-    chips, rows, lanes = out_ref.shape
+def scan_kernel(parts, side_ref, term_ref, out_hbm, out_ref, sems):
+    along, chip_rows, rows, lanes = out_ref.shape
     rows = rows // 2
-    block = 8
 
     def some(i, states):
-        for k in range(block):
-            at = i * block + k
-            decays = log_decays(term_ref[at, 2 * rows :])
+        for k in range(along):
+            decays = log_decays(term_ref[k, i, 2 * rows :])
             after = []
             for side in range(2):
                 span = slice(side * rows, (side + 1) * rows)
-                out_ref[at, span] = states[side].astype(BF16)
-                after.append(jnp.exp(decays[side]) * states[side] + term_ref[at, span].astype(F32))
+                out_ref[k, i, span] = states[side].astype(BF16)
+                after.append(jnp.exp(decays[side]) * states[side] + term_ref[k, i, span].astype(F32))
             states = tuple(after)
         return states
 
-    lax.fori_loop(0, chips // block, some, (jnp.zeros((rows, lanes), F32),) * 2)
+    states = (jnp.zeros((rows, lanes), F32),) * 2
+    size = chip_rows // parts
+    for part in range(parts):
+        states = lax.fori_loop(part * size, (part + 1) * size, some, states)
+        part_copy(parts, part, out_ref, out_hbm, sems).start()
+    for part in range(parts):
+        part_copy(parts, part, out_ref, out_hbm, sems).wait()
 
 
 def entries(side, terms):
-    chips, rows, lanes = terms.shape
-    return on_chip(scan_kernel, (chips, rows - EXTRA, lanes), side, terms)
+    along, chip_rows, rows, lanes = terms.shape
+    return off_chip(scan_kernel, (along, chip_rows, rows - EXTRA, lanes), side, terms)
 
 
 def read_kernel(channels, mine, side_ref, cum_ref, c_ref, diagonal_ref, held_ref, *rest):
@@ -478,8 +507,8 @@
 
 def shards(inputs, log_decay, write_vectors, read_vectors):
     chips = lax.axis_size("seq") * lax.axis_size("z")
-    pieces_n = 8
-    pieces_c = chips // pieces_n
+    pieces_n = lax.axis_size("z")
+    pieces_c = lax.axis_size("seq")
     own_side = lax.axis_index("c").astype(jnp.int32).reshape(1)
     other_side = 1 - own_side
     swap = [(0, 1), (1, 0)]
@@ -491,11 +520,12 @@
     kept = second_states(own_side, cumulative, inputs, write_vectors, pieces_n, pieces_c)
     term = joined(own_side, kept, came)
 
-    terms = lax.all_to_all(term.reshape((chips,) + term.shape[2:]), ("seq", "z"), 0, 0, tiled=True)
+    terms = lax.all_to_all(term.reshape((chips,) + term.shape[2:]), ("z", "seq"), 0, 0, tiled=True)
     diagonal_own = diagonals(own_side, cumulative, inputs, write_vectors, read_vectors)
     terms, diagonal_own = lax.optimization_barrier((terms, diagonal_own))
 
-    held = lax.all_to_all(entries(own_side, terms), ("seq", "z"), 0, 0, tiled=True)
+    held = entries(own_side, terms.reshape(term.shape))
+    held = lax.all_to_all(held.reshape((chips,) + held.shape[2:]), ("z", "seq"), 0, 0, tiled=True)
     diagonal_other = diagonals(other_side, cumulative, inputs, write_vectors, read_vectors)
     held, diagonal_other = lax.optimization_barrier((held, diagonal_other))
     held = held.reshape(term.shape[:2] + held.shape[1:])

time: 115 us -> 114 us (level)
  waiting for transfers between devices: 44.1 us -> 41.1 us
  starting transfers between devices: 27.8 us -> 30.1 us
  local copies, waits for them, and re-layouts: 18.3 us -> 16.7 us
  Pallas kernels: 23.9 us -> 25.4 us
    all_to_all x2, waiting for transfers between devices: 43.8 us -> 40.7 us  [the longest x1 23.6 us: shards(): lax.all_to_all(term.reshape((chips,) + term.shape[2:]), ('z', 'seq'), 0,...]
    pallas_call x0 -> x2, Pallas kernels: none -> 2.58 us  [off_chip(): pl.pallas_call(functools.partial(kernel, parts), in_specs=[pl.BlockSpec(m...]
    all_to_all x2, starting transfers between devices: 20.1 us -> 22.2 us  [the longest x1 13.8 us: shards(): lax.all_to_all(term.reshape((chips,) + term.shape[2:]), ('z', 'seq'), 0,...]
    unnamed x32 -> x28, local copies, waits for them, and re-layouts: 18.3 us -> 16.7 us
where the time goes in v2:
time: 114 us
  waiting for transfers between devices  41.1 us (36%)
  starting transfers between devices  30.1 us (26%)
  Pallas kernels  25.4 us (22%)
  local copies, waits for them, and re-layouts  16.7 us (15%)
    all_to_all x1, waiting for transfers between devices, shards(): lax.all_to_all(term.reshape((chips,) + term.shape[2:]), ('z', 'seq'), 0,...  23.6 us
    all_to_all x1, waiting for transfers between devices, shards(): lax.all_to_all(held.reshape((chips,) + held.shape[2:]), ('z', 'seq'), 0,...  17.2 us
    unnamed x28, local copies, waits for them, and re-layouts  16.7 us
    all_to_all x1, starting transfers between devices, shards(): lax.all_to_all(term.reshape((chips,) + term.shape[2:]), ('z', 'seq'), 0,...  13.8 us
    pallas_call x2, Pallas kernels, diagonals(): pl.pallas_call(lambda *refs: diagonal_kernel(width // heads, *refs), in_s...  9.53 us
    all_to_all x1, starting transfers between devices, shards(): lax.all_to_all(held.reshape((chips,) + held.shape[2:]), ('z', 'seq'), 0,...  8.38 us
    pallas_call x1, Pallas kernels, first_states(): pl.pallas_call(lambda *refs: first_kernel(width // heads, *refs), in_spec...  5.95 us
    pallas_call x2, Pallas kernels, outputs(): pl.pallas_call(lambda *refs: read_kernel(width // heads, came is not None...  4.96 us
  transfers between devices with their start and end apart: 4, of which 3 were waited for; matrix products, arithmetic and copies ran while one was open for 0% of the time, Pallas kernels for 13%

profile of v2, /device:TPU:1, one launch (start us, length us, event | category | flops | bytes accessed | tf_op | source)
XLA Modules:
  0.0 113.6 jit_solution(1709352503992622167)
XLA Ops:
  0.0 5.9 %shard_map.46 = (f32[320,128]{1,0:T(8,128)S(1)}, bf16[8,16,40,128]{3,2,1,0:T(8,128)(2,1)S(1)}, bf16[320,8192]{1,0:T(8,128)(2,1)S(1)}, bf16[320,1024]{1,0:T(8,128)(2,1)S(1)}) custom-call(s32[1]{0:T(128)S(6)} %sub.3.refs_0_, f32[320,128]{1,0:T(8,128)} %refs_1_.1, bf16[320,8192]{1,0:T(8,128)(2,1)} %refs_2_.3, bf16[320,1024]{1,0:T(8,128)(2,1)} %refs_3_.1), custom_call_target="tpu_custom_call" | custom-call | flops 1342177280 | bytes 10485760 | tf_op jit(solution)/shard_map/pallas_call | solution.py:182
  6.0 3.3 %collective-permute-start = (bf16[8,16,40,128]{3,2,1,0:T(8,128)(2,1)S(1)}, bf16[8,16,40,128]{3,2,1,0:T(8,128)(2,1)S(1)}, u32[]{:S(2)}, u32[]{:S(2)}) collective-permute-start(bf16[8,16,40,128]{3,2,1,0:T(8,128)(2,1)S(1)} %get-tuple-element.16), channel_id=1, source_target_pairs={{0,1},{1,0},{2,3},{3,2},{4,5},{5,4},{6,7},{7,6},{8,9},{9,8},{10,11... | collective-permute-start | bytes 3932168 | tf_op jit(solution)/shard_map/ppermute | solution.py:519
  9.3 2.3 %shard_map.47.kept_ref = bf16[8,16,40,128]{3,2,1,0:T(8,128)(2,1)S(1)} custom-call(s32[1]{0:T(128)} %bitcast.refs_0_.side_ref, f32[320,128]{1,0:T(8,128)S(1)} %get-tuple-element.13.refs_1_, bf16[320,8192]{1,0:T(8,128)(2,1)S(1)} %get-tuple-element.14.refs_2_, bf16[320,1024]{1,0:T(8,128)(2,1)S(1)} %get-tuple-element.15.refs_3_), custom_call_target="tpu_custom_call" | custom-call | flops 1342177280 | bytes 2621440 | tf_op jit(solution)/shard_map/pallas_call | solution.py:207
  11.6 0.3 collective-permute-done.came_ref.refs_5_
  12.0 1.3 %shard_map.48 = bf16[8,16,40,128]{3,2,1,0:T(8,128)(2,1)} custom-call(s32[1]{0:T(128)} %bitcast.refs_0_.side_ref, bf16[8,16,40,128]{3,2,1,0:T(8,128)(2,1)S(1)} %shard_map.47.kept_ref, bf16[8,16,40,128]{3,2,1,0:T(8,128)(2,1)S(1)} %collective-permute-done.came_ref.refs_5_), custom_call_target="tpu_custom_call" | custom-call | tf_op jit(solution)/shard_map/pallas_call | solution.py:265
  13.3 1.0 copy-done.6
  14.4 13.8 %all-to-all-start = ((bf16[128,40,128]{2,1,0:T(8,128)(2,1)}), bf16[128,40,128]{2,1,0:T(8,128)(2,1)S(1)}, u32[]{:S(2)}, u32[]{:S(2)}) async-start(bf16[128,40,128]{2,1,0:T(8,128)(2,1)} %bitcast.10), calls=%async_computation | async-start | bytes 2621440 | tf_op jit(solution)/shard_map/all_to_all | solution.py:523
  28.2 2.5 %copy-done.4 = bf16[320,8192]{1,0:T(8,128)(2,1)S(1)} copy-done((bf16[320,8192]{1,0:T(8,128)(2,1)S(1)}, bf16[320,8192]{1,0:T(8,128)(2,1)}, u32[]{:S(2)}) %copy-start.4) | copy-done | bytes 5242904
  30.6 1.1 copy-done.10
  31.7 4.8 %shard_map.49.refs_3_ = f32[320,4096]{1,0:T(8,128)S(1)} custom-call(s32[1]{0:T(128)} %bitcast.refs_0_.side_ref, f32[320,128]{1,0:T(8,128)S(1)} %get-tuple-element.13.refs_1_, bf16[320,8192]{1,0:T(8,128)(2,1)S(1)} %copy-done.4, bf16[320,1024]{1,0:T(8,128)(2,1)S(1)} %copy-done.10, bf16[320,1024]{1,0:T(8,128)(2,1)S(1)} %copy-done.8), custom_call_target="tpu_custom_call" | custom-call | flops 838860800 | bytes 7864320 | tf_op jit(solution)/shard_map/pallas_call | solution.py:382
  36.5 2.3 %copy-done.1 = f32[320,4096]{1,0:T(8,128)} copy-done((f32[320,4096]{1,0:T(8,128)}, f32[320,4096]{1,0:T(8,128)S(1)}, u32[]{:S(2)}) %copy-start.1) | copy-done | bytes 5242904
  38.8 23.6 %all-to-all-done = bf16[128,40,128]{2,1,0:T(8,128)(2,1)S(1)} async-done(((bf16[128,40,128]{2,1,0:T(8,128)(2,1)}), bf16[128,40,128]{2,1,0:T(8,128)(2,1)S(1)}, u32[]{:S(2)}, u32[]{:S(2)}) %all-to-all-start) | async-done | bytes 1310752 | tf_op jit(solution)/shard_map/all_to_all | solution.py:523
  62.4 1.3 %shard_map.50 = bf16[8,16,32,128]{3,2,1,0:T(8,128)(2,1)} custom-call(s32[1]{0:T(128)} %bitcast.refs_0_.side_ref, bf16[8,16,40,128]{3,2,1,0:T(8,128)(2,1)S(1)} %bitcast.9), custom_call_target="tpu_custom_call" | custom-call | tf_op jit(solution)/shard_map/pallas_call | solution.py:265
  63.7 8.4 %all-to-all-start.1 = ((bf16[128,32,128]{2,1,0:T(8,128)(2,1)}), bf16[128,32,128]{2,1,0:T(8,128)(2,1)S(1)}, u32[]{:S(2)}, u32[]{:S(2)}) async-start(bf16[128,32,128]{2,1,0:T(8,128)(2,1)} %bitcast.11), calls=%async_computation.1 | async-start | bytes 2097152 | tf_op jit(solution)/shard_map/all_to_all | solution.py:528
  72.1 2.5 %copy-done.5 = bf16[320,8192]{1,0:T(8,128)(2,1)S(1)} copy-done((bf16[320,8192]{1,0:T(8,128)(2,1)S(1)}, bf16[320,8192]{1,0:T(8,128)(2,1)}, u32[]{:S(2)}) %copy-start.5) | copy-done | bytes 5242904
  74.6 1.1 copy-done.11
  75.7 4.8 %shard_map.51.refs_3_ = f32[320,4096]{1,0:T(8,128)S(1)} custom-call(s32[1]{0:T(128)S(6)} %sub.3.refs_0_, f32[320,128]{1,0:T(8,128)S(1)} %get-tuple-element.13.refs_1_, bf16[320,8192]{1,0:T(8,128)(2,1)S(1)} %copy-done.5, bf16[320,1024]{1,0:T(8,128)(2,1)S(1)} %copy-done.11, bf16[320,1024]{1,0:T(8,128)(2,1)S(1)} %copy-done.8), custom_call_target="tpu_custom_call" | custom-call | flops 838860800 | bytes 7864320 | tf_op jit(solution)/shard_map/pallas_call | solution.py:382
  80.4 2.4 %copy-done = f32[320,4096]{1,0:T(8,128)} copy-done((f32[320,4096]{1,0:T(8,128)}, f32[320,4096]{1,0:T(8,128)S(1)}, u32[]{:S(2)}) %copy-start) | copy-done | bytes 5242904
  82.8 17.2 %all-to-all-done.1 = bf16[128,32,128]{2,1,0:T(8,128)(2,1)S(1)} async-done(((bf16[128,32,128]{2,1,0:T(8,128)(2,1)}), bf16[128,32,128]{2,1,0:T(8,128)(2,1)S(1)}, u32[]{:S(2)}, u32[]{:S(2)}) %all-to-all-start.1) | async-done | bytes 1048608 | tf_op jit(solution)/shard_map/all_to_all | solution.py:528
  100.0 4.6 %collective-permute-start.1 = (bf16[8,16,32,128]{3,2,1,0:T(8,128)(2,1)S(1)}, bf16[8,16,32,128]{3,2,1,0:T(8,128)(2,1)S(1)}, u32[]{:S(2)}, u32[]{:S(2)}) collective-permute-start(bf16[8,16,32,128]{3,2,1,0:T(8,128)(2,1)S(1)} %shard_map.52), channel_id=1, source_target_pairs={{0,1},{1,0},{2,3},{3,2},{4,5},{5,4},{6,7},{7,6},{8,9},{9,8},{10,11... | collective-permute-start | bytes 3145736 | tf_op jit(solution)/shard_map/ppermute | solution.py:533
  104.7 2.5 %copy-done.2 = f32[320,4096]{1,0:T(8,128)S(1)} copy-done((f32[320,4096]{1,0:T(8,128)S(1)}, f32[320,4096]{1,0:T(8,128)}, u32[]{:S(2)}) %copy-start.2) | copy-done | bytes 5242904
  107.1 1.3 %copy-done.7 = bf16[8,16,40,128]{3,2,1,0:T(8,128)(2,1)S(1)} copy-done((bf16[8,16,40,128]{3,2,1,0:T(8,128)(2,1)S(1)}, bf16[8,16,40,128]{3,2,1,0:T(8,128)(2,1)}, u32[]{:S(2)}) %copy-start.7) | copy-done | bytes 1310744
  108.5 2.5 %shard_map.53.refs_5_ = bf16[320,8192]{1,0:T(8,128)(2,1)} custom-call(s32[1]{0:T(128)} %bitcast.refs_0_.side_ref, f32[320,128]{1,0:T(8,128)S(1)} %get-tuple-element.13.refs_1_, bf16[320,1024]{1,0:T(8,128)(2,1)S(1)} %copy-done.8, f32[320,4096]{1,0:T(8,128)S(1)} %copy-done.2, bf16[8,16,32,128]{3,2,1,0:T(8,128)(2,1)S(1)} %bitcast.6, ...), custom_call_target="tpu_custom_call" | custom-call | flops 671088640 | bytes 5242880 | tf_op jit(solution)/shard_map/pallas_call | solution.py:487
  111.0 2.5 %shard_map.54 = bf16[320,8192]{1,0:T(8,128)(2,1)} custom-call(s32[1]{0:T(128)S(6)} %sub.3.refs_0_, f32[320,128]{1,0:T(8,128)S(1)} %get-tuple-element.13.refs_1_, bf16[320,1024]{1,0:T(8,128)(2,1)S(1)} %copy-done.8, f32[320,4096]{1,0:T(8,128)S(1)} %bitcast.8, ...), custom_call_target="tpu_custom_call", output_to_operand_aliasing={{}: (5, {})} | custom-call | flops 671088640 | bytes 5242880 | tf_op jit(solution)/shard_map/pallas_call | solution.py:487
  (22 shorter events, 0.1 us)
Async XLA Ops:
  6.0 7.3 %copy-start.3 = (bf16[320,8192]{1,0:T(8,128)(2,1)}, bf16[320,8192]{1,0:T(8,128)(2,1)S(1)}, u32[]{:S(2)}) copy-start(bf16[320,8192]{1,0:T(8,128)(2,1)S(1)} %get-tuple-element.14.refs_2_) | copy-start | bytes 15728644
  6.0 7.3 %copy-start.9 = (bf16[320,1024]{1,0:T(8,128)(2,1)}, bf16[320,1024]{1,0:T(8,128)(2,1)S(1)}, u32[]{:S(2)}) copy-start(bf16[320,1024]{1,0:T(8,128)(2,1)S(1)} %get-tuple-element.15.refs_3_) | copy-start | bytes 1966084
  6.0 6.0 %collective-permute-start = (bf16[8,16,40,128]{3,2,1,0:T(8,128)(2,1)S(1)}, bf16[8,16,40,128]{3,2,1,0:T(8,128)(2,1)S(1)}, u32[]{:S(2)}, u32[]{:S(2)}) collective-permute-start(bf16[8,16,40,128]{3,2,1,0:T(8,128)(2,1)S(1)} %get-tuple-element.16), channel_id=1, source_target_pairs={{0,1},{1,0},{2,3},{3,2},{4,5},{5,4},{6,7},{7,6},{8,9},{9,8},{10,11... | collective-permute-start | bytes 3932168 | tf_op jit(solution)/shard_map/ppermute | solution.py:519
  9.3 18.8 %copy-start.8 = (bf16[320,1024]{1,0:T(8,128)(2,1)S(1)}, bf16[320,1024]{1,0:T(8,128)(2,1)}, u32[]{:S(2)}) copy-start(bf16[320,1024]{1,0:T(8,128)(2,1)} %refs_2_.5) | copy-start | bytes 1966084
  13.3 1.1 copy-start.6
  14.4 48.1 %all-to-all-start = ((bf16[128,40,128]{2,1,0:T(8,128)(2,1)}), bf16[128,40,128]{2,1,0:T(8,128)(2,1)S(1)}, u32[]{:S(2)}, u32[]{:S(2)}) async-start(bf16[128,40,128]{2,1,0:T(8,128)(2,1)} %bitcast.10), calls=%async_computation | async-start | bytes 2621440 | tf_op jit(solution)/shard_map/all_to_all | solution.py:523
  28.2 2.5 %copy-start.4 = (bf16[320,8192]{1,0:T(8,128)(2,1)S(1)}, bf16[320,8192]{1,0:T(8,128)(2,1)}, u32[]{:S(2)}) copy-start(bf16[320,8192]{1,0:T(8,128)(2,1)} %copy-done.3) | copy-start | bytes 15728644
  30.6 1.1 copy-start.10
  36.5 2.3 %copy-start.1 = (f32[320,4096]{1,0:T(8,128)}, f32[320,4096]{1,0:T(8,128)S(1)}, u32[]{:S(2)}) copy-start(f32[320,4096]{1,0:T(8,128)S(1)} %shard_map.49.refs_3_) | copy-start | bytes 15728644
  63.7 36.3 %all-to-all-start.1 = ((bf16[128,32,128]{2,1,0:T(8,128)(2,1)}), bf16[128,32,128]{2,1,0:T(8,128)(2,1)S(1)}, u32[]{:S(2)}, u32[]{:S(2)}) async-start(bf16[128,32,128]{2,1,0:T(8,128)(2,1)} %bitcast.11), calls=%async_computation.1 | async-start | bytes 2097152 | tf_op jit(solution)/shard_map/all_to_all | solution.py:528
  72.1 2.5 %copy-start.5 = (bf16[320,8192]{1,0:T(8,128)(2,1)S(1)}, bf16[320,8192]{1,0:T(8,128)(2,1)}, u32[]{:S(2)}) copy-start(bf16[320,8192]{1,0:T(8,128)(2,1)} %copy-done.3) | copy-start | bytes 15728644
  74.6 1.1 copy-start.11
  80.4 2.4 %copy-start = (f32[320,4096]{1,0:T(8,128)}, f32[320,4096]{1,0:T(8,128)S(1)}, u32[]{:S(2)}) copy-start(f32[320,4096]{1,0:T(8,128)S(1)} %shard_map.51.refs_3_) | copy-start | bytes 15728644
  100.0 11.0 %slice-start = ((s8[5242880]{0:T(1024)(128)(4,1)}), s8[4194304]{0:T(1024)(128)(4,1)S(1)}, s32[]{:S(2)}) async-start(s8[5242880]{0:T(1024)(128)(4,1)} %bitcast.7), calls=%async_computation.2 | async-start | bytes 8388608
  100.0 11.0 %slice-start.1 = ((s8[5242880]{0:T(1024)(128)(4,1)}), s8[1048576]{0:T(1024)(128)(4,1)S(1)}, s32[]{:S(2)}) async-start(s8[5242880]{0:T(1024)(128)(4,1)} %bitcast.7), calls=%async_computation.3 | async-start | bytes 2097152
  100.0 10.9 %collective-permute-start.1 = (bf16[8,16,32,128]{3,2,1,0:T(8,128)(2,1)S(1)}, bf16[8,16,32,128]{3,2,1,0:T(8,128)(2,1)S(1)}, u32[]{:S(2)}, u32[]{:S(2)}) collective-permute-start(bf16[8,16,32,128]{3,2,1,0:T(8,128)(2,1)S(1)} %shard_map.52), channel_id=1, source_target_pairs={{0,1},{1,0},{2,3},{3,2},{4,5},{5,4},{6,7},{7,6},{8,9},{9,8},{10,11... | collective-permute-start | bytes 3145736 | tf_op jit(solution)/shard_map/ppermute | solution.py:533
  104.7 2.5 %copy-start.2 = (f32[320,4096]{1,0:T(8,128)S(1)}, f32[320,4096]{1,0:T(8,128)}, u32[]{:S(2)}) copy-start(f32[320,4096]{1,0:T(8,128)} %copy-done.1) | copy-start | bytes 15728644
  107.1 1.3 %copy-start.7 = (bf16[8,16,40,128]{3,2,1,0:T(8,128)(2,1)S(1)}, bf16[8,16,40,128]{3,2,1,0:T(8,128)(2,1)}, u32[]{:S(2)}) copy-start(bf16[8,16,40,128]{3,2,1,0:T(8,128)(2,1)} %copy-done.6) | copy-start | bytes 3932164

commit v3 on v2

--- a/solution.py
+++ b/solution.py
@@ -12,6 +12,7 @@
 LOG2E = math.log2(math.e)
 VMEM_LIMIT = 16 * 1024 * 1024
 EXTRA = 8
+THIN = 4
 F32 = jnp.float32
 BF16 = jnp.bfloat16
 
@@ -64,8 +65,7 @@
 
 
 def pack_decays(first, second):
-    parts = [part.astype(F32) for whole in (first, second) for part in split_three(whole)]
-    parts.append(jnp.zeros((EXTRA - len(parts), first.shape[1]), F32))
+    parts = [part.astype(F32) for whole in (first, second) for part in split_two(whole)]
     return jnp.concatenate(parts, axis=0).astype(BF16)
 
 
@@ -228,11 +228,12 @@
                 span = slice(k * rows, (k + 1) * rows)
                 decay = jnp.exp(after[k])
                 for i in range(blocks_n):
-                    out_ref[i, j, span] = (
-                        decay * first_ref[i, j, span].astype(F32) + second_ref[i, j, span].astype(F32)
-                    ).astype(BF16)
+                    both = decay * first_ref[i, j, span].astype(F32) + second_ref[i, j, span].astype(F32)
+                    for r in range(rows // THIN):
+                        thin = both[r * THIN : (r + 1) * THIN]
+                        out_ref[i, j, k * (rows // THIN) + r] = thin.astype(BF16)
             for i in range(blocks_n):
-                out_ref[i, j, 2 * rows :] = extra
+                out_ref[i, j, 2 * rows // THIN] = extra
             if (j + 1) % (blocks_c // parts) == 0:
                 part_copy(parts, j * parts // blocks_c, out_ref, out_hbm, sems).start()
 
@@ -279,7 +280,9 @@
 
 
 def joined(side, kept, came):
-    return off_chip(join_kernel, kept.shape, side, kept, came)
+    blocks_n, blocks_c, rows, lanes = kept.shape
+    shape = (blocks_n, blocks_c, (rows - EXTRA) // THIN + 1, THIN, lanes)
+    return off_chip(join_kernel, shape, side, kept, came)
 
 
 def give_kernel(side_ref, held_ref, kept_ref, out_ref):
@@ -404,12 +407,15 @@
 
     def some(i, states):
         for k in range(along):
-            decays = log_decays(term_ref[k, i, 2 * rows :])
+            logs = term_ref[k, i, 2 * rows // THIN].astype(F32)
             after = []
             for side in range(2):
                 span = slice(side * rows, (side + 1) * rows)
                 out_ref[k, i, span] = states[side].astype(BF16)
-                after.append(jnp.exp(decays[side]) * states[side] + term_ref[k, i, span].astype(F32))
+                decay = jnp.exp(logs[2 * side : 2 * side + 1] + logs[2 * side + 1 : 2 * side + 2])
+                first = side * (rows // THIN)
+                term = [term_ref[k, i, first + r].astype(F32) for r in range(rows // THIN)]
+                after.append(decay * states[side] + jnp.concatenate(term, axis=0))
             states = tuple(after)
         return states
 
@@ -423,8 +429,8 @@
 
 
 def entries(side, terms):
-    along, chip_rows, rows, lanes = terms.shape
-    return off_chip(scan_kernel, (along, chip_rows, rows - EXTRA, lanes), side, terms)
+    along, chip_rows, thins, _, lanes = terms.shape
+    return off_chip(scan_kernel, (along, chip_rows, (thins - 1) * THIN, lanes), side, terms)
 
 
 def read_kernel(channels, mine, side_ref, cum_ref, c_ref, diagonal_ref, held_ref, *rest):

time: 114 us -> 111 us (0.974)
  waiting for transfers between devices: 41.1 us -> 38.4 us
    all_to_all x1, waiting for transfers between devices: 23.6 us -> 21.1 us  [shards(): lax.all_to_all(term.reshape((chips,) + term.shape[2:]), ('z', 'seq'), 0,...]
where the time goes in v3:
time: 111 us
  waiting for transfers between devices  38.4 us (35%)
  starting transfers between devices  29.9 us (27%)
  Pallas kernels  25.6 us (23%)
  local copies, waits for them, and re-layouts  16.7 us (15%)
    all_to_all x1, waiting for transfers between devices, shards(): lax.all_to_all(term.reshape((chips,) + term.shape[2:]), ('z', 'seq'), 0,...  21.1 us
    all_to_all x1, waiting for transfers between devices, shards(): lax.all_to_all(held.reshape((chips,) + held.shape[2:]), ('z', 'seq'), 0,...  16.9 us
    unnamed x28, local copies, waits for them, and re-layouts  16.7 us
    all_to_all x1, starting transfers between devices, shards(): lax.all_to_all(term.reshape((chips,) + term.shape[2:]), ('z', 'seq'), 0,...  13.8 us
    pallas_call x2, Pallas kernels, diagonals(): pl.pallas_call(lambda *refs: diagonal_kernel(width // heads, *refs), in_s...  9.54 us
    all_to_all x1, starting transfers between devices, shards(): lax.all_to_all(held.reshape((chips,) + held.shape[2:]), ('z', 'seq'), 0,...  7.97 us
    pallas_call x1, Pallas kernels, first_states(): pl.pallas_call(lambda *refs: first_kernel(width // heads, *refs), in_spec...  5.95 us
    pallas_call x2, Pallas kernels, outputs(): pl.pallas_call(lambda *refs: read_kernel(width // heads, came is not None...  4.96 us
  transfers between devices with their start and end apart: 4, of which 3 were waited for; matrix products, arithmetic and copies ran while one was open for 0% of the time, Pallas kernels for 13%

profile of v3, /device:TPU:1, one launch (start us, length us, event | category | flops | bytes accessed | tf_op | source)
XLA Modules:
  0.0 111.0 jit_solution(12496817260621755121)
XLA Ops:
  0.0 5.9 %shard_map.46 = (f32[320,128]{1,0:T(8,128)S(1)}, bf16[8,16,40,128]{3,2,1,0:T(8,128)(2,1)S(1)}, bf16[320,8192]{1,0:T(8,128)(2,1)S(1)}, bf16[320,1024]{1,0:T(8,128)(2,1)S(1)}) custom-call(s32[1]{0:T(128)S(6)} %sub.3.refs_0_, f32[320,128]{1,0:T(8,128)} %refs_1_.1, bf16[320,8192]{1,0:T(8,128)(2,1)} %refs_2_.3, bf16[320,1024]{1,0:T(8,128)(2,1)} %refs_3_.1), custom_call_target="tpu_custom_call" | custom-call | flops 1342177280 | bytes 10485760 | tf_op jit(solution)/shard_map/pallas_call | solution.py:182
  6.0 3.3 %collective-permute-start = (bf16[8,16,40,128]{3,2,1,0:T(8,128)(2,1)S(1)}, bf16[8,16,40,128]{3,2,1,0:T(8,128)(2,1)S(1)}, u32[]{:S(2)}, u32[]{:S(2)}) collective-permute-start(bf16[8,16,40,128]{3,2,1,0:T(8,128)(2,1)S(1)} %get-tuple-element.16), channel_id=1, source_target_pairs={{0,1},{1,0},{2,3},{3,2},{4,5},{5,4},{6,7},{7,6},{8,9},{9,8},{10,11... | collective-permute-start | bytes 3932168 | tf_op jit(solution)/shard_map/ppermute | solution.py:525
  9.3 2.3 %shard_map.47.kept_ref = bf16[8,16,40,128]{3,2,1,0:T(8,128)(2,1)S(1)} custom-call(s32[1]{0:T(128)} %bitcast.refs_0_.side_ref, f32[320,128]{1,0:T(8,128)S(1)} %get-tuple-element.13.refs_1_, bf16[320,8192]{1,0:T(8,128)(2,1)S(1)} %get-tuple-element.14.refs_2_, bf16[320,1024]{1,0:T(8,128)(2,1)S(1)} %get-tuple-element.15.refs_3_), custom_call_target="tpu_custom_call" | custom-call | flops 1342177280 | bytes 2621440 | tf_op jit(solution)/shard_map/pallas_call | solution.py:207
  11.6 0.3 collective-permute-done.came_ref.refs_5_
  12.0 1.4 %shard_map.48 = bf16[8,16,9,4,128]{4,3,2,1,0:T(4,128)(2,1)} custom-call(s32[1]{0:T(128)} %bitcast.refs_0_.side_ref, bf16[8,16,40,128]{3,2,1,0:T(8,128)(2,1)S(1)} %shard_map.47.kept_ref, bf16[8,16,40,128]{3,2,1,0:T(8,128)(2,1)S(1)} %collective-permute-done.came_ref.refs_5_), custom_call_target="tpu_custom_call" | custom-call | tf_op jit(solution)/shard_map/pallas_call | solution.py:266
  13.4 1.0 copy-done.6
  14.5 13.8 %all-to-all-start = ((bf16[128,9,4,128]{3,2,1,0:T(4,128)(2,1)}), bf16[128,9,4,128]{3,2,1,0:T(4,128)(2,1)S(1)}, u32[]{:S(2)}, u32[]{:S(2)}) async-start(bf16[128,9,4,128]{3,2,1,0:T(4,128)(2,1)} %bitcast.10), calls=%async_computation | async-start | bytes 2359296 | tf_op jit(solution)/shard_map/all_to_all | solution.py:529
  28.3 2.5 %copy-done.4 = bf16[320,8192]{1,0:T(8,128)(2,1)S(1)} copy-done((bf16[320,8192]{1,0:T(8,128)(2,1)S(1)}, bf16[320,8192]{1,0:T(8,128)(2,1)}, u32[]{:S(2)}) %copy-start.4) | copy-done | bytes 5242904
  30.7 1.1 copy-done.10
  31.8 4.8 %shard_map.49.refs_3_ = f32[320,4096]{1,0:T(8,128)S(1)} custom-call(s32[1]{0:T(128)} %bitcast.refs_0_.side_ref, f32[320,128]{1,0:T(8,128)S(1)} %get-tuple-element.13.refs_1_, bf16[320,8192]{1,0:T(8,128)(2,1)S(1)} %copy-done.4, bf16[320,1024]{1,0:T(8,128)(2,1)S(1)} %copy-done.10, bf16[320,1024]{1,0:T(8,128)(2,1)S(1)} %copy-done.8), custom_call_target="tpu_custom_call" | custom-call | flops 838860800 | bytes 7864320 | tf_op jit(solution)/shard_map/pallas_call | solution.py:385
  36.6 2.3 %copy-done.1 = f32[320,4096]{1,0:T(8,128)} copy-done((f32[320,4096]{1,0:T(8,128)}, f32[320,4096]{1,0:T(8,128)S(1)}, u32[]{:S(2)}) %copy-start.1) | copy-done | bytes 5242904
  38.9 21.1 %all-to-all-done = bf16[128,9,4,128]{3,2,1,0:T(4,128)(2,1)S(1)} async-done(((bf16[128,9,4,128]{3,2,1,0:T(4,128)(2,1)}), bf16[128,9,4,128]{3,2,1,0:T(4,128)(2,1)S(1)}, u32[]{:S(2)}, u32[]{:S(2)}) %all-to-all-start) | async-done | bytes 1179680 | tf_op jit(solution)/shard_map/all_to_all | solution.py:529
  60.0 1.4 %shard_map.50 = bf16[8,16,32,128]{3,2,1,0:T(8,128)(2,1)} custom-call(s32[1]{0:T(128)} %bitcast.refs_0_.side_ref, bf16[8,16,9,4,128]{4,3,2,1,0:T(4,128)(2,1)S(1)} %bitcast.9), custom_call_target="tpu_custom_call" | custom-call | tf_op jit(solution)/shard_map/pallas_call | solution.py:266
  61.4 8.0 %all-to-all-start.1 = ((bf16[128,32,128]{2,1,0:T(8,128)(2,1)}), bf16[128,32,128]{2,1,0:T(8,128)(2,1)S(1)}, u32[]{:S(2)}, u32[]{:S(2)}) async-start(bf16[128,32,128]{2,1,0:T(8,128)(2,1)} %bitcast.11), calls=%async_computation.1 | async-start | bytes 2097152 | tf_op jit(solution)/shard_map/all_to_all | solution.py:534
  69.4 2.5 %copy-done.5 = bf16[320,8192]{1,0:T(8,128)(2,1)S(1)} copy-done((bf16[320,8192]{1,0:T(8,128)(2,1)S(1)}, bf16[320,8192]{1,0:T(8,128)(2,1)}, u32[]{:S(2)}) %copy-start.5) | copy-done | bytes 5242904
  71.9 1.1 copy-done.11
  73.0 4.8 %shard_map.51.refs_3_ = f32[320,4096]{1,0:T(8,128)S(1)} custom-call(s32[1]{0:T(128)S(6)} %sub.3.refs_0_, f32[320,128]{1,0:T(8,128)S(1)} %get-tuple-element.13.refs_1_, bf16[320,8192]{1,0:T(8,128)(2,1)S(1)} %copy-done.5, bf16[320,1024]{1,0:T(8,128)(2,1)S(1)} %copy-done.11, bf16[320,1024]{1,0:T(8,128)(2,1)S(1)} %copy-done.8), custom_call_target="tpu_custom_call" | custom-call | flops 838860800 | bytes 7864320 | tf_op jit(solution)/shard_map/pallas_call | solution.py:385
  77.8 2.4 %copy-done = f32[320,4096]{1,0:T(8,128)} copy-done((f32[320,4096]{1,0:T(8,128)}, f32[320,4096]{1,0:T(8,128)S(1)}, u32[]{:S(2)}) %copy-start) | copy-done | bytes 5242904
  80.1 16.9 %all-to-all-done.1 = bf16[128,32,128]{2,1,0:T(8,128)(2,1)S(1)} async-done(((bf16[128,32,128]{2,1,0:T(8,128)(2,1)}), bf16[128,32,128]{2,1,0:T(8,128)(2,1)S(1)}, u32[]{:S(2)}, u32[]{:S(2)}) %all-to-all-start.1) | async-done | bytes 1048608 | tf_op jit(solution)/shard_map/all_to_all | solution.py:534
  97.1 4.8 %collective-permute-start.1 = (bf16[8,16,32,128]{3,2,1,0:T(8,128)(2,1)S(1)}, bf16[8,16,32,128]{3,2,1,0:T(8,128)(2,1)S(1)}, u32[]{:S(2)}, u32[]{:S(2)}) collective-permute-start(bf16[8,16,32,128]{3,2,1,0:T(8,128)(2,1)S(1)} %shard_map.52), channel_id=1, source_target_pairs={{0,1},{1,0},{2,3},{3,2},{4,5},{5,4},{6,7},{7,6},{8,9},{9,8},{10,11... | collective-permute-start | bytes 3145736 | tf_op jit(solution)/shard_map/ppermute | solution.py:539
  102.0 2.5 %copy-done.2 = f32[320,4096]{1,0:T(8,128)S(1)} copy-done((f32[320,4096]{1,0:T(8,128)S(1)}, f32[320,4096]{1,0:T(8,128)}, u32[]{:S(2)}) %copy-start.2) | copy-done | bytes 5242904
  104.5 1.3 %copy-done.7 = bf16[8,16,40,128]{3,2,1,0:T(8,128)(2,1)S(1)} copy-done((bf16[8,16,40,128]{3,2,1,0:T(8,128)(2,1)S(1)}, bf16[8,16,40,128]{3,2,1,0:T(8,128)(2,1)}, u32[]{:S(2)}) %copy-start.7) | copy-done | bytes 1310744
  105.8 2.5 %shard_map.53.refs_5_ = bf16[320,8192]{1,0:T(8,128)(2,1)} custom-call(s32[1]{0:T(128)} %bitcast.refs_0_.side_ref, f32[320,128]{1,0:T(8,128)S(1)} %get-tuple-element.13.refs_1_, bf16[320,1024]{1,0:T(8,128)(2,1)S(1)} %copy-done.8, f32[320,4096]{1,0:T(8,128)S(1)} %copy-done.2, bf16[8,16,32,128]{3,2,1,0:T(8,128)(2,1)S(1)} %bitcast.6, ...), custom_call_target="tpu_custom_call" | custom-call | flops 671088640 | bytes 5242880 | tf_op jit(solution)/shard_map/pallas_call | solution.py:493
  108.3 2.5 %shard_map.54 = bf16[320,8192]{1,0:T(8,128)(2,1)} custom-call(s32[1]{0:T(128)S(6)} %sub.3.refs_0_, f32[320,128]{1,0:T(8,128)S(1)} %get-tuple-element.13.refs_1_, bf16[320,1024]{1,0:T(8,128)(2,1)S(1)} %copy-done.8, f32[320,4096]{1,0:T(8,128)S(1)} %bitcast.8, ...), custom_call_target="tpu_custom_call", output_to_operand_aliasing={{}: (5, {})} | custom-call | flops 671088640 | bytes 5242880 | tf_op jit(solution)/shard_map/pallas_call | solution.py:493
  (22 shorter events, 0.1 us)
Async XLA Ops:
  6.0 7.4 %copy-start.3 = (bf16[320,8192]{1,0:T(8,128)(2,1)}, bf16[320,8192]{1,0:T(8,128)(2,1)S(1)}, u32[]{:S(2)}) copy-start(bf16[320,8192]{1,0:T(8,128)(2,1)S(1)} %get-tuple-element.14.refs_2_) | copy-start | bytes 15728644
  6.0 7.4 %copy-start.9 = (bf16[320,1024]{1,0:T(8,128)(2,1)}, bf16[320,1024]{1,0:T(8,128)(2,1)S(1)}, u32[]{:S(2)}) copy-start(bf16[320,1024]{1,0:T(8,128)(2,1)S(1)} %get-tuple-element.15.refs_3_) | copy-start | bytes 1966084
  6.0 6.0 %collective-permute-start = (bf16[8,16,40,128]{3,2,1,0:T(8,128)(2,1)S(1)}, bf16[8,16,40,128]{3,2,1,0:T(8,128)(2,1)S(1)}, u32[]{:S(2)}, u32[]{:S(2)}) collective-permute-start(bf16[8,16,40,128]{3,2,1,0:T(8,128)(2,1)S(1)} %get-tuple-element.16), channel_id=1, source_target_pairs={{0,1},{1,0},{2,3},{3,2},{4,5},{5,4},{6,7},{7,6},{8,9},{9,8},{10,11... | collective-permute-start | bytes 3932168 | tf_op jit(solution)/shard_map/ppermute | solution.py:525
  9.3 18.9 %copy-start.8 = (bf16[320,1024]{1,0:T(8,128)(2,1)S(1)}, bf16[320,1024]{1,0:T(8,128)(2,1)}, u32[]{:S(2)}) copy-start(bf16[320,1024]{1,0:T(8,128)(2,1)} %refs_2_.5) | copy-start | bytes 1966084
  13.4 1.1 copy-start.6
  14.5 45.6 %all-to-all-start = ((bf16[128,9,4,128]{3,2,1,0:T(4,128)(2,1)}), bf16[128,9,4,128]{3,2,1,0:T(4,128)(2,1)S(1)}, u32[]{:S(2)}, u32[]{:S(2)}) async-start(bf16[128,9,4,128]{3,2,1,0:T(4,128)(2,1)} %bitcast.10), calls=%async_computation | async-start | bytes 2359296 | tf_op jit(solution)/shard_map/all_to_all | solution.py:529
  28.2 2.5 %copy-start.4 = (bf16[320,8192]{1,0:T(8,128)(2,1)S(1)}, bf16[320,8192]{1,0:T(8,128)(2,1)}, u32[]{:S(2)}) copy-start(bf16[320,8192]{1,0:T(8,128)(2,1)} %copy-done.3) | copy-start | bytes 15728644
  30.7 1.1 copy-start.10
  36.6 2.3 %copy-start.1 = (f32[320,4096]{1,0:T(8,128)}, f32[320,4096]{1,0:T(8,128)S(1)}, u32[]{:S(2)}) copy-start(f32[320,4096]{1,0:T(8,128)S(1)} %shard_map.49.refs_3_) | copy-start | bytes 15728644
  61.4 35.6 %all-to-all-start.1 = ((bf16[128,32,128]{2,1,0:T(8,128)(2,1)}), bf16[128,32,128]{2,1,0:T(8,128)(2,1)S(1)}, u32[]{:S(2)}, u32[]{:S(2)}) async-start(bf16[128,32,128]{2,1,0:T(8,128)(2,1)} %bitcast.11), calls=%async_computation.1 | async-start | bytes 2097152 | tf_op jit(solution)/shard_map/all_to_all | solution.py:534
  69.4 2.5 %copy-start.5 = (bf16[320,8192]{1,0:T(8,128)(2,1)S(1)}, bf16[320,8192]{1,0:T(8,128)(2,1)}, u32[]{:S(2)}) copy-start(bf16[320,8192]{1,0:T(8,128)(2,1)} %copy-done.3) | copy-start | bytes 15728644
  71.9 1.1 copy-start.11
  77.7 2.4 %copy-start = (f32[320,4096]{1,0:T(8,128)}, f32[320,4096]{1,0:T(8,128)S(1)}, u32[]{:S(2)}) copy-start(f32[320,4096]{1,0:T(8,128)S(1)} %shard_map.51.refs_3_) | copy-start | bytes 15728644
  97.1 11.2 %slice-start = ((s8[5242880]{0:T(1024)(128)(4,1)}), s8[4194304]{0:T(1024)(128)(4,1)S(1)}, s32[]{:S(2)}) async-start(s8[5242880]{0:T(1024)(128)(4,1)} %bitcast.7), calls=%async_computation.2 | async-start | bytes 8388608
  97.1 11.2 %slice-start.1 = ((s8[5242880]{0:T(1024)(128)(4,1)}), s8[1048576]{0:T(1024)(128)(4,1)S(1)}, s32[]{:S(2)}) async-start(s8[5242880]{0:T(1024)(128)(4,1)} %bitcast.7), calls=%async_computation.3 | async-start | bytes 2097152
  97.1 11.1 %collective-permute-start.1 = (bf16[8,16,32,128]{3,2,1,0:T(8,128)(2,1)S(1)}, bf16[8,16,32,128]{3,2,1,0:T(8,128)(2,1)S(1)}, u32[]{:S(2)}, u32[]{:S(2)}) collective-permute-start(bf16[8,16,32,128]{3,2,1,0:T(8,128)(2,1)S(1)} %shard_map.52), channel_id=1, source_target_pairs={{0,1},{1,0},{2,3},{3,2},{4,5},{5,4},{6,7},{7,6},{8,9},{9,8},{10,11... | collective-permute-start | bytes 3145736 | tf_op jit(solution)/shard_map/ppermute | solution.py:539
  102.0 2.5 %copy-start.2 = (f32[320,4096]{1,0:T(8,128)S(1)}, f32[320,4096]{1,0:T(8,128)}, u32[]{:S(2)}) copy-start(f32[320,4096]{1,0:T(8,128)} %copy-done.1) | copy-start | bytes 15728644
  104.5 1.3 %copy-start.7 = (bf16[8,16,40,128]{3,2,1,0:T(8,128)(2,1)S(1)}, bf16[8,16,40,128]{3,2,1,0:T(8,128)(2,1)}, u32[]{:S(2)}) copy-start(bf16[8,16,40,128]{3,2,1,0:T(8,128)(2,1)} %copy-done.6) | copy-start | bytes 3932164

commit v4 on v3

--- a/solution.py
+++ b/solution.py
@@ -434,8 +434,26 @@
 
 
 def read_kernel(channels, mine, side_ref, cum_ref, c_ref, diagonal_ref, held_ref, *rest):
+    if mine:
+        late_diagonal, late_came = diagonal_ref, rest[0]
+        rest, (diagonal_ref, came_ref, diagonal_sems, came_sems) = rest[:-4], rest[-4:]
     out_hbm, grown_ref, pick_ref, out_ref, sems = rest[-5:]
     half, _, columns = out_ref.shape
+    bring = []
+    for turn in range(half if mine else 0):
+        size = came_ref.shape[1] // half
+        part = pl.ds(turn * size, size)
+        pair = (
+            pltpu.make_async_copy(late_came.at[:, part], came_ref.at[:, part], came_sems.at[turn]),
+            pltpu.make_async_copy(
+                group_columns(late_diagonal, turn, columns),
+                group_columns(diagonal_ref, turn, columns),
+                diagonal_sems.at[turn],
+            ),
+        )
+        for copy in pair:
+            copy.start()
+        bring.append(pair)
     state_size = c_ref.shape[1] // G
     grown_ref[...] = jnp.exp(cum_ref[...])
     pick_ref[...] = head_columns(columns, channels, cum_ref.shape[1])
@@ -449,6 +467,8 @@
         readers = group_columns(c_ref, group, state_size)[...]
         if mine:
             readers = jnp.concatenate([readers, readers], axis=1)
+        for copy in bring[turn] if mine else ():
+            copy.wait()
         for j in range(count):
             sides = []
             for k in range(2):
@@ -456,7 +476,6 @@
                 span = slice(k * rows, (k + 1) * rows)
                 held = jnp.concatenate([held_ref[i, at, span] for i in range(blocks_n)], axis=0)
                 if mine:
-                    came_ref = rest[0]
                     second = side_ref[0] == 1
                     came = jnp.concatenate([came_ref[i, at, span] for i in range(blocks_n)], axis=0)
                     logs = log_decays(came_ref[0, at, 2 * rows :])[k]
@@ -483,9 +502,18 @@
     in_specs = [SCALAR] + [WHOLE] * 4
     args = [side, cumulative, read_vectors, diagonal, held]
     aliases = {}
+    extra = []
     if came is not None:
-        in_specs.append(WHOLE)
-        args.append(came)
+        in_specs[3] = LEFT
+        args[3] = pltpu.with_memory_space_constraint(diagonal, pltpu.HBM)
+        in_specs.append(LEFT)
+        args.append(pltpu.with_memory_space_constraint(came, pltpu.HBM))
+        extra = [
+            pltpu.VMEM(diagonal.shape, F32),
+            pltpu.VMEM(came.shape, BF16),
+            pltpu.SemaphoreType.DMA((half,)),
+            pltpu.SemaphoreType.DMA((half,)),
+        ]
     if done is not None:
         in_specs.append(LEFT)
         aliases = {len(args): 0}
@@ -499,7 +527,7 @@
             pltpu.VMEM((2 * heads, columns), BF16),
             pltpu.VMEM((half, length, columns), BF16),
             pltpu.SemaphoreType.DMA((half,)),
-        ],
+        ] + extra,
         out_shape=jax.ShapeDtypeStruct((length, width), BF16),
         input_output_aliases=aliases,
         compiler_params=pltpu.CompilerParams(vmem_limit_bytes=VMEM_LIMIT),

time: 111 us -> 110 us (level)
  local copies, waits for them, and re-layouts: 16.7 us -> 12.9 us
  Pallas kernels: 25.6 us -> 28.4 us
    unnamed x28 -> x24, local copies, waits for them, and re-layouts: 16.7 us -> 12.9 us
    pallas_call x2, Pallas kernels: 4.96 us -> 7.76 us  [outputs(): pl.pallas_call(lambda *refs: read_kernel(width // heads, came is not None...]
  transfers between devices with their start and end apart: 4 -> 4, of which waited for: 3 -> 3; matrix products, arithmetic and copies ran while one was open for 0% -> 0% of each run, Pallas kernels for 13% -> 16%
where the time goes in v4:
time: 110 us
  waiting for transfers between devices  38.4 us (35%)
  starting transfers between devices  29.9 us (27%)
  Pallas kernels  28.4 us (26%)
  local copies, waits for them, and re-layouts  12.9 us (12%)
    all_to_all x1, waiting for transfers between devices, shards(): lax.all_to_all(term.reshape((chips,) + term.shape[2:]), ('z', 'seq'), 0,...  21.1 us
    all_to_all x1, waiting for transfers between devices, shards(): lax.all_to_all(held.reshape((chips,) + held.shape[2:]), ('z', 'seq'), 0,...  17 us
    all_to_all x1, starting transfers between devices, shards(): lax.all_to_all(term.reshape((chips,) + term.shape[2:]), ('z', 'seq'), 0,...  13.8 us
    unnamed x24, local copies, waits for them, and re-layouts  12.9 us
    pallas_call x2, Pallas kernels, diagonals(): pl.pallas_call(lambda *refs: diagonal_kernel(width // heads, *refs), in_s...  9.54 us
    all_to_all x1, starting transfers between devices, shards(): lax.all_to_all(held.reshape((chips,) + held.shape[2:]), ('z', 'seq'), 0,...  7.97 us
    pallas_call x2, Pallas kernels, outputs(): pl.pallas_call(lambda *refs: read_kernel(width // heads, came is not None...  7.76 us
    pallas_call x1, Pallas kernels, first_states(): pl.pallas_call(lambda *refs: first_kernel(width // heads, *refs), in_spec...  5.95 us
  transfers between devices with their start and end apart: 4, of which 3 were waited for; matrix products, arithmetic and copies ran while one was open for 0% of the time, Pallas kernels for 16%

profile of v4, /device:TPU:1, one launch (start us, length us, event | category | flops | bytes accessed | tf_op | source)
XLA Modules:
  0.0 110.0 jit_solution(3323392568983573440)
XLA Ops:
  0.0 5.9 %shard_map.46 = (f32[320,128]{1,0:T(8,128)S(1)}, bf16[8,16,40,128]{3,2,1,0:T(8,128)(2,1)S(1)}, bf16[320,8192]{1,0:T(8,128)(2,1)S(1)}, bf16[320,1024]{1,0:T(8,128)(2,1)S(1)}) custom-call(s32[1]{0:T(128)S(6)} %sub.3.refs_0_, f32[320,128]{1,0:T(8,128)} %refs_1_.1, bf16[320,8192]{1,0:T(8,128)(2,1)} %refs_2_.3, bf16[320,1024]{1,0:T(8,128)(2,1)} %refs_3_.1), custom_call_target="tpu_custom_call" | custom-call | flops 1342177280 | bytes 10485760 | tf_op jit(solution)/shard_map/pallas_call | solution.py:182
  6.0 3.3 %collective-permute-start = (bf16[8,16,40,128]{3,2,1,0:T(8,128)(2,1)S(1)}, bf16[8,16,40,128]{3,2,1,0:T(8,128)(2,1)S(1)}, u32[]{:S(2)}, u32[]{:S(2)}) collective-permute-start(bf16[8,16,40,128]{3,2,1,0:T(8,128)(2,1)S(1)} %get-tuple-element.16), channel_id=1, source_target_pairs={{0,1},{1,0},{2,3},{3,2},{4,5},{5,4},{6,7},{7,6},{8,9},{9,8},{10,11... | collective-permute-start | bytes 3932168 | tf_op jit(solution)/shard_map/ppermute | solution.py:553
  9.3 2.3 %shard_map.47.kept_ref = bf16[8,16,40,128]{3,2,1,0:T(8,128)(2,1)S(1)} custom-call(s32[1]{0:T(128)} %bitcast.refs_0_.side_ref, f32[320,128]{1,0:T(8,128)S(1)} %get-tuple-element.13.refs_1_, bf16[320,8192]{1,0:T(8,128)(2,1)S(1)} %get-tuple-element.14.refs_2_, bf16[320,1024]{1,0:T(8,128)(2,1)S(1)} %get-tuple-element.15.refs_3_), custom_call_target="tpu_custom_call" | custom-call | flops 1342177280 | bytes 2621440 | tf_op jit(solution)/shard_map/pallas_call | solution.py:207
  11.6 0.3 collective-permute-done.came_ref.refs_5_
  12.0 1.4 %shard_map.48 = bf16[8,16,9,4,128]{4,3,2,1,0:T(4,128)(2,1)} custom-call(s32[1]{0:T(128)} %bitcast.refs_0_.side_ref, bf16[8,16,40,128]{3,2,1,0:T(8,128)(2,1)S(1)} %shard_map.47.kept_ref, bf16[8,16,40,128]{3,2,1,0:T(8,128)(2,1)S(1)} %collective-permute-done.came_ref.refs_5_), custom_call_target="tpu_custom_call" | custom-call | tf_op jit(solution)/shard_map/pallas_call | solution.py:266
  13.4 1.1 copy-done.5
  14.5 13.8 %all-to-all-start = ((bf16[128,9,4,128]{3,2,1,0:T(4,128)(2,1)}), bf16[128,9,4,128]{3,2,1,0:T(4,128)(2,1)S(1)}, u32[]{:S(2)}, u32[]{:S(2)}) async-start(bf16[128,9,4,128]{3,2,1,0:T(4,128)(2,1)} %bitcast.10), calls=%async_computation | async-start | bytes 2359296 | tf_op jit(solution)/shard_map/all_to_all | solution.py:557
  28.3 0.0 copy-start.3
  28.3 2.5 %copy-done.3 = bf16[320,8192]{1,0:T(8,128)(2,1)S(1)} copy-done((bf16[320,8192]{1,0:T(8,128)(2,1)S(1)}, bf16[320,8192]{1,0:T(8,128)(2,1)}, u32[]{:S(2)}) %copy-start.3) | copy-done | bytes 5242904
  30.8 1.1 copy-done.8
  31.8 4.8 %shard_map.49.refs_3_ = f32[320,4096]{1,0:T(8,128)S(1)} custom-call(s32[1]{0:T(128)} %bitcast.refs_0_.side_ref, f32[320,128]{1,0:T(8,128)S(1)} %get-tuple-element.13.refs_1_, bf16[320,8192]{1,0:T(8,128)(2,1)S(1)} %copy-done.3, bf16[320,1024]{1,0:T(8,128)(2,1)S(1)} %copy-done.8, bf16[320,1024]{1,0:T(8,128)(2,1)S(1)} %copy-done.6), custom_call_target="tpu_custom_call" | custom-call | flops 838860800 | bytes 7864320 | tf_op jit(solution)/shard_map/pallas_call | solution.py:385
  36.6 2.3 %copy-done.1 = f32[320,4096]{1,0:T(8,128)} copy-done((f32[320,4096]{1,0:T(8,128)}, f32[320,4096]{1,0:T(8,128)S(1)}, u32[]{:S(2)}) %copy-start.1) | copy-done | bytes 5242904
  39.0 21.1 %all-to-all-done = bf16[128,9,4,128]{3,2,1,0:T(4,128)(2,1)S(1)} async-done(((bf16[128,9,4,128]{3,2,1,0:T(4,128)(2,1)}), bf16[128,9,4,128]{3,2,1,0:T(4,128)(2,1)S(1)}, u32[]{:S(2)}, u32[]{:S(2)}) %all-to-all-start) | async-done | bytes 1179680 | tf_op jit(solution)/shard_map/all_to_all | solution.py:557
  60.0 1.4 %shard_map.50 = bf16[8,16,32,128]{3,2,1,0:T(8,128)(2,1)} custom-call(s32[1]{0:T(128)} %bitcast.refs_0_.side_ref, bf16[8,16,9,4,128]{4,3,2,1,0:T(4,128)(2,1)S(1)} %bitcast.9), custom_call_target="tpu_custom_call" | custom-call | tf_op jit(solution)/shard_map/pallas_call | solution.py:266
  61.4 8.0 %all-to-all-start.1 = ((bf16[128,32,128]{2,1,0:T(8,128)(2,1)}), bf16[128,32,128]{2,1,0:T(8,128)(2,1)S(1)}, u32[]{:S(2)}, u32[]{:S(2)}) async-start(bf16[128,32,128]{2,1,0:T(8,128)(2,1)} %bitcast.11), calls=%async_computation.1 | async-start | bytes 2097152 | tf_op jit(solution)/shard_map/all_to_all | solution.py:562
  69.4 2.5 %copy-done.4 = bf16[320,8192]{1,0:T(8,128)(2,1)S(1)} copy-done((bf16[320,8192]{1,0:T(8,128)(2,1)S(1)}, bf16[320,8192]{1,0:T(8,128)(2,1)}, u32[]{:S(2)}) %copy-start.4) | copy-done | bytes 5242904
  71.9 1.1 copy-done.9
  73.0 4.8 %shard_map.51.refs_3_ = f32[320,4096]{1,0:T(8,128)S(1)} custom-call(s32[1]{0:T(128)S(6)} %sub.3.refs_0_, f32[320,128]{1,0:T(8,128)S(1)} %get-tuple-element.13.refs_1_, bf16[320,8192]{1,0:T(8,128)(2,1)S(1)} %copy-done.4, bf16[320,1024]{1,0:T(8,128)(2,1)S(1)} %copy-done.9, bf16[320,1024]{1,0:T(8,128)(2,1)S(1)} %copy-done.6), custom_call_target="tpu_custom_call" | custom-call | flops 838860800 | bytes 7864320 | tf_op jit(solution)/shard_map/pallas_call | solution.py:385
  77.8 2.3 %copy-done = f32[320,4096]{1,0:T(8,128)} copy-done((f32[320,4096]{1,0:T(8,128)}, f32[320,4096]{1,0:T(8,128)S(1)}, u32[]{:S(2)}) %copy-start) | copy-done | bytes 5242904
  80.1 17.0 %all-to-all-done.1 = bf16[128,32,128]{2,1,0:T(8,128)(2,1)S(1)} async-done(((bf16[128,32,128]{2,1,0:T(8,128)(2,1)}), bf16[128,32,128]{2,1,0:T(8,128)(2,1)S(1)}, u32[]{:S(2)}, u32[]{:S(2)}) %all-to-all-start.1) | async-done | bytes 1048608 | tf_op jit(solution)/shard_map/all_to_all | solution.py:562
  97.1 0.1 shard_map.52
  97.2 4.8 %collective-permute-start.1 = (bf16[8,16,32,128]{3,2,1,0:T(8,128)(2,1)S(1)}, bf16[8,16,32,128]{3,2,1,0:T(8,128)(2,1)S(1)}, u32[]{:S(2)}, u32[]{:S(2)}) collective-permute-start(bf16[8,16,32,128]{3,2,1,0:T(8,128)(2,1)S(1)} %shard_map.52), channel_id=1, source_target_pairs={{0,1},{1,0},{2,3},{3,2},{4,5},{5,4},{6,7},{7,6},{8,9},{9,8},{10,11... | collective-permute-start | bytes 3145736 | tf_op jit(solution)/shard_map/ppermute | solution.py:567
  102.0 5.3 %shard_map.53.refs_5_ = bf16[320,8192]{1,0:T(8,128)(2,1)} custom-call(s32[1]{0:T(128)} %bitcast.refs_0_.side_ref, f32[320,128]{1,0:T(8,128)S(1)} %get-tuple-element.13.refs_1_, bf16[320,1024]{1,0:T(8,128)(2,1)S(1)} %copy-done.6, f32[320,4096]{1,0:T(8,128)} %copy-done.1, bf16[8,16,32,128]{3,2,1,0:T(8,128)(2,1)S(1)} %bitcast.6, bf16[8,16,40,128]{3,2,1,0:T(8,128)(2,1)} %copy-done.5), custom_call_target="tpu_custom_call" | custom-call | flops 671088640 | bytes 5242880 | tf_op jit(solution)/shard_map/pallas_call | solution.py:521
  107.3 2.5 %shard_map.54 = bf16[320,8192]{1,0:T(8,128)(2,1)} custom-call(s32[1]{0:T(128)S(6)} %sub.3.refs_0_, f32[320,128]{1,0:T(8,128)S(1)} %get-tuple-element.13.refs_1_, bf16[320,1024]{1,0:T(8,128)(2,1)S(1)} %copy-done.6, f32[320,4096]{1,0:T(8,128)S(1)} %bitcast.8, ...), custom_call_target="tpu_custom_call", output_to_operand_aliasing={{}: (5, {})} | custom-call | flops 671088640 | bytes 5242880 | tf_op jit(solution)/shard_map/pallas_call | solution.py:521
  (18 shorter events, 0.0 us)
Async XLA Ops:
  6.0 7.4 %copy-start.2 = (bf16[320,8192]{1,0:T(8,128)(2,1)}, bf16[320,8192]{1,0:T(8,128)(2,1)S(1)}, u32[]{:S(2)}) copy-start(bf16[320,8192]{1,0:T(8,128)(2,1)S(1)} %get-tuple-element.14.refs_2_) | copy-start | bytes 15728644
  6.0 7.4 %copy-start.7 = (bf16[320,1024]{1,0:T(8,128)(2,1)}, bf16[320,1024]{1,0:T(8,128)(2,1)S(1)}, u32[]{:S(2)}) copy-start(bf16[320,1024]{1,0:T(8,128)(2,1)S(1)} %get-tuple-element.15.refs_3_) | copy-start | bytes 1966084
  6.0 6.0 %collective-permute-start = (bf16[8,16,40,128]{3,2,1,0:T(8,128)(2,1)S(1)}, bf16[8,16,40,128]{3,2,1,0:T(8,128)(2,1)S(1)}, u32[]{:S(2)}, u32[]{:S(2)}) collective-permute-start(bf16[8,16,40,128]{3,2,1,0:T(8,128)(2,1)S(1)} %get-tuple-element.16), channel_id=1, source_target_pairs={{0,1},{1,0},{2,3},{3,2},{4,5},{5,4},{6,7},{7,6},{8,9},{9,8},{10,11... | collective-permute-start | bytes 3932168 | tf_op jit(solution)/shard_map/ppermute | solution.py:553
  9.3 19.0 %copy-start.6 = (bf16[320,1024]{1,0:T(8,128)(2,1)S(1)}, bf16[320,1024]{1,0:T(8,128)(2,1)}, u32[]{:S(2)}) copy-start(bf16[320,1024]{1,0:T(8,128)(2,1)} %refs_2_.5) | copy-start | bytes 1966084
  13.4 1.1 copy-start.5
  14.5 45.6 %all-to-all-start = ((bf16[128,9,4,128]{3,2,1,0:T(4,128)(2,1)}), bf16[128,9,4,128]{3,2,1,0:T(4,128)(2,1)S(1)}, u32[]{:S(2)}, u32[]{:S(2)}) async-start(bf16[128,9,4,128]{3,2,1,0:T(4,128)(2,1)} %bitcast.10), calls=%async_computation | async-start | bytes 2359296 | tf_op jit(solution)/shard_map/all_to_all | solution.py:557
  28.3 2.5 %copy-start.3 = (bf16[320,8192]{1,0:T(8,128)(2,1)S(1)}, bf16[320,8192]{1,0:T(8,128)(2,1)}, u32[]{:S(2)}) copy-start(bf16[320,8192]{1,0:T(8,128)(2,1)} %copy-done.2) | copy-start | bytes 15728644
  30.8 1.1 copy-start.8
  36.6 2.3 %copy-start.1 = (f32[320,4096]{1,0:T(8,128)}, f32[320,4096]{1,0:T(8,128)S(1)}, u32[]{:S(2)}) copy-start(f32[320,4096]{1,0:T(8,128)S(1)} %shard_map.49.refs_3_) | copy-start | bytes 15728644
  61.4 35.6 %all-to-all-start.1 = ((bf16[128,32,128]{2,1,0:T(8,128)(2,1)}), bf16[128,32,128]{2,1,0:T(8,128)(2,1)S(1)}, u32[]{:S(2)}, u32[]{:S(2)}) async-start(bf16[128,32,128]{2,1,0:T(8,128)(2,1)} %bitcast.11), calls=%async_computation.1 | async-start | bytes 2097152 | tf_op jit(solution)/shard_map/all_to_all | solution.py:562
  69.4 2.5 %copy-start.4 = (bf16[320,8192]{1,0:T(8,128)(2,1)S(1)}, bf16[320,8192]{1,0:T(8,128)(2,1)}, u32[]{:S(2)}) copy-start(bf16[320,8192]{1,0:T(8,128)(2,1)} %copy-done.2) | copy-start | bytes 15728644
  71.9 1.1 copy-start.9
  77.8 2.4 %copy-start = (f32[320,4096]{1,0:T(8,128)}, f32[320,4096]{1,0:T(8,128)S(1)}, u32[]{:S(2)}) copy-start(f32[320,4096]{1,0:T(8,128)S(1)} %shard_map.51.refs_3_) | copy-start | bytes 15728644
  97.1 10.2 %slice-start = ((s8[5242880]{0:T(1024)(128)(4,1)}), s8[1048576]{0:T(1024)(128)(4,1)S(1)}, s32[]{:S(2)}) async-start(s8[5242880]{0:T(1024)(128)(4,1)} %bitcast.7), calls=%async_computation.2 | async-start | bytes 2097152
  97.2 10.2 %slice-start.1 = ((s8[5242880]{0:T(1024)(128)(4,1)}), s8[4194304]{0:T(1024)(128)(4,1)S(1)}, s32[]{:S(2)}) async-start(s8[5242880]{0:T(1024)(128)(4,1)} %bitcast.7), calls=%async_computation.3 | async-start | bytes 8388608
  97.2 10.1 %collective-permute-start.1 = (bf16[8,16,32,128]{3,2,1,0:T(8,128)(2,1)S(1)}, bf16[8,16,32,128]{3,2,1,0:T(8,128)(2,1)S(1)}, u32[]{:S(2)}, u32[]{:S(2)}) collective-permute-start(bf16[8,16,32,128]{3,2,1,0:T(8,128)(2,1)S(1)} %shard_map.52), channel_id=1, source_target_pairs={{0,1},{1,0},{2,3},{3,2},{4,5},{5,4},{6,7},{7,6},{8,9},{9,8},{10,11... | collective-permute-start | bytes 3145736 | tf_op jit(solution)/shard_map/ppermute | solution.py:567
